TPU v7x, 256 devices: a whole 4x4x8 slice. The times are simulated.
256 devices in a mesh: dp: 256 (over y, z, x, core).
Axes of the slice: x: 4, y: 4, z: 8, core: 2. Of those that a mesh axis runs over, the one named last changes fastest.
Arguments:
- tokens: bfloat16 [98304, 2560], P('dp'), may hold values from -24 to 24
- segment_ids: int32 [256, 384], P('dp'), may hold values from 0 to 3, never falling along the last dimension, each value on 1 to 192 neighbouring positions
- grad_out: bfloat16 [98304, 2560], P('dp'), may hold values from -24 to 24
- norm_gain: bfloat16 [2560], P('dp'), may hold values from 0.099609375 to 1.8984375
- w_qkv: bfloat16 [2560, 768], P('dp'), may hold values from -0.125 to 0.125
- w_out: bfloat16 [512, 2560], P(None, 'dp'), may hold values from -0.25 to 0.25
Outputs:
- output: bfloat16 [98304, 2560], P('dp')
- grad_tokens: bfloat16 [98304, 2560], P('dp')
- grad_qkv: float32 [2560, 768], P('dp')
- grad_wout: float32 [512, 2560], P(None, 'dp')
- grad_gain: float32 [2560], P('dp')
Inputs may be any that keep to these rules, and one draw needn't show every extreme that they name: `segment_ids`: ids do not fall along a row; every id occurs in each row, no document spans more than 192 positions, and one spans exactly 192.
All inputs are finite; a program needn't handle non-finite values.
Results may differ from a plain program's by a relative error of at most 0.024.
Values may be sent and summed in bfloat16 or wider, within the bound.
A program may use at most 128 MiB of HBM per device.

v0:
```python
from functools import partial

import jax
import jax.numpy as jnp
from jax import lax
from jax.sharding import PartitionSpec as P

Q_HEADS = 4
HEAD_DIM = 128


norm_eps = 1e-06
rope_base = 1000000.0


def rms_scale(values):
    return values * lax.rsqrt(jnp.mean(values * values, axis=-1, keepdims=True) + norm_eps)


def rotate(vectors, cosine, sine):
    half = vectors.shape[-1] // 2
    first = vectors[..., :half]
    second = vectors[..., half:]
    return jnp.concatenate(
        [first * cosine - second * sine, second * cosine + first * sine], axis=-1
    )


def document_layout(segment):
    length = segment.shape[0]
    places = jnp.arange(length, dtype=jnp.int32)
    matching = segment[:, None] == segment[None, :]
    first_place = jnp.min(jnp.where(matching, places[None, :], length), axis=1)
    positions = (places - first_place).astype(jnp.float32)
    allowed = matching & (places[None, :] <= places[:, None])
    return (positions, allowed)


def attention_core(projected, segment):
    length = projected.shape[0]
    width = Q_HEADS * HEAD_DIM
    queries = projected[:, :width].reshape(length, Q_HEADS, HEAD_DIM)
    key_head = projected[:, width : width + HEAD_DIM]
    value_head = projected[:, width + HEAD_DIM :]
    positions, allowed = document_layout(segment)
    half = HEAD_DIM // 2
    inverse = rope_base ** (-2.0 * jnp.arange(half, dtype=jnp.float32) / HEAD_DIM)
    angles = positions[:, None] * inverse[None, :]
    cosine = jnp.cos(angles)
    sine = jnp.sin(angles)
    queries = rotate(rms_scale(queries), cosine[:, None, :], sine[:, None, :]).astype(jnp.bfloat16)
    key_head = rotate(rms_scale(key_head), cosine, sine).astype(jnp.bfloat16)
    value_head = value_head.astype(jnp.bfloat16)
    scores = jnp.einsum(
        "thd,sd->hts", queries, key_head, preferred_element_type=jnp.float32
    ) * HEAD_DIM ** (-0.5)
    weights = jnp.where(allowed[None], jnp.exp(scores), 0.0)
    probs = (weights / jnp.sum(weights, axis=-1, keepdims=True)).astype(jnp.bfloat16)
    mixed = jnp.einsum("hts,sd->thd", probs, value_head, preferred_element_type=jnp.float32)
    return mixed.reshape(length, width).astype(jnp.bfloat16)


def section_attention(tokens, norm_gain, w_qkv, segment):
    scaled = rms_scale(tokens.astype(jnp.float32))
    normed = (scaled * norm_gain.astype(jnp.float32)).astype(jnp.bfloat16)
    projected = jnp.dot(normed, w_qkv, preferred_element_type=jnp.float32)
    return attention_core(projected, segment)


def section_output(tokens, mixed, w_out):
    update = jnp.dot(mixed, w_out, preferred_element_type=jnp.float32)
    return (tokens.astype(jnp.float32) + update).astype(jnp.bfloat16)


def widen(values):
    return lax.optimization_barrier(values).astype(jnp.float32)


def per_device(tokens, segment_ids, grad_out, norm_gain, w_qkv, w_out):
    segment = segment_ids[0]
    scaled = rms_scale(tokens.astype(jnp.float32))
    gain_piece = lax.all_gather(norm_gain, "dp", axis=0, tiled=True)
    weight_piece = lax.all_gather(w_qkv, "dp", axis=0, tiled=True)
    normed = (scaled * gain_piece.astype(jnp.float32)).astype(jnp.bfloat16)
    projected = jnp.dot(normed, weight_piece, preferred_element_type=jnp.float32)
    mixed = attention_core(projected, segment)
    residual = tokens.astype(jnp.float32)
    forward_output = (
        residual
        + jnp.dot(
            mixed,
            lax.all_gather(w_out, "dp", axis=1, tiled=True),
            preferred_element_type=jnp.float32,
        )
    ).astype(jnp.bfloat16)
    full_gain, full_qkv, full_out = (
        lax.all_gather(norm_gain, "dp", axis=0, tiled=True),
        lax.all_gather(w_qkv, "dp", axis=0, tiled=True),
        lax.all_gather(w_out, "dp", axis=1, tiled=True),
    )
    mixed_again, pull_attention = jax.vjp(
        partial(section_attention, segment=segment), tokens, full_gain, full_qkv
    )
    recomputed, pull_output = jax.vjp(section_output, tokens, mixed_again, full_out)
    grad_residual, grad_mixed, grad_weight_out = pull_output(grad_out)
    grad_normpath, grad_gain, grad_weight_qkv = pull_attention(grad_mixed)
    qkv_share, out_share, gain_share = (
        lax.psum_scatter(widen(grad_weight_qkv), "dp", scatter_dimension=0, tiled=True),
        lax.psum_scatter(widen(grad_weight_out), "dp", scatter_dimension=1, tiled=True),
        lax.psum_scatter(widen(grad_gain), "dp", scatter_dimension=0, tiled=True),
    )
    return (forward_output, grad_residual + grad_normpath, qkv_share, out_share, gain_share)


def solution(mesh):
    return jax.shard_map(
        per_device,
        mesh=mesh,
        in_specs=(
            P("dp", None),
            P("dp", None),
            P("dp", None),
            P("dp"),
            P("dp", None),
            P(None, "dp"),
        ),
        out_specs=(P("dp", None), P("dp", None), P("dp", None), P(None, "dp"), P("dp")),
        check_vma=False,
    )
```

profile of v0, /device:TPU:1, one launch (start us, length us, event | category | flops | bytes accessed | tf_op | source)
XLA Modules:
  0.0 468.3 jit_solution(16476245390499765240)
XLA Ops:
  9.5 81.7 %all-reduce.7 = bf16[2560]{0:T(1024)(128)(2,1)S(1)} all-reduce(bf16[2560]{0:T(1024)(128)(2,1)S(1)} %dynamic-update-slice), channel_id=1, replica_groups=mesh['dp'=256] {'dp'}, use_global_device_ids=true, to_apply=%add.7 | all-reduce | flops 2560 | bytes 10240
  92.9 0.9 copy.74
  94.4 2.0 fusion.6
  97.0 33.9 %all-gather.7.cloned.1.call-done = bf16[256,10,512]{2,1,0:T(8,128)(2,1)} async-done(((bf16[1,10,512]{2,1,0:T(8,128)(2,1)}), bf16[256,10,512]{2,1,0:T(8,128)(2,1)}) %all-gather.7.cloned.1.call-update) | async-done | bytes 2621456 | tf_op jit(solution)/shard_map/all_gather | solution.py:92
  131.0 6.2 %reshape.196 = bf16[2560,512]{1,0:T(8,128)(2,1)} reshape(bf16[256,10,512]{2,1,0:T(8,128)(2,1)} %all-gather.7.cloned.1.call-done) | data formatting | bytes 5242880
  137.1 2.9 convolution_convert_fusion.5
  140.0 1.0 copy.90
  141.0 107.1 %all-gather.5.cloned.1.call-done = bf16[256,10,768]{2,1,0:T(8,128)(2,1)} async-done(((bf16[1,10,768]{2,1,0:T(8,128)(2,1)}), bf16[256,10,768]{2,1,0:T(8,128)(2,1)}) %all-gather.5.cloned.1.call-update) | async-done | bytes 3932176 | tf_op jit(solution)/shard_map/all_gather | solution.py:83
  248.1 8.2 %reshape.194 = bf16[2560,768]{1,0:T(8,128)(2,1)} reshape(bf16[256,10,768]{2,1,0:T(8,128)(2,1)} %all-gather.5.cloned.1.call-done) | data formatting | bytes 7864320
  256.3 3.8 fusion.28
  261.9 1.1 reshape.188
  263.0 1.6 multiply_reduce_fusion
  265.5 1.0 slice_multiply_fusion
  269.4 1.0 fusion.14
  270.4 1.2 fusion.17
  271.6 1.1 fusion.20
  276.6 3.6 fusion.4
  280.2 4.2 convolution_convert_fusion
  284.4 2.6 fusion.2
  286.9 1.5 convolution_convert_fusion.1
  288.5 163.4 %all-reduce.13 = (f32[2560,768]{1,0:T(8,128)}, f32[512,2560]{1,0:T(8,128)}, f32[2560]{0:T(1024)S(1)}) all-reduce(bf16[2560,768]{1,0:T(8,128)(2,1)} %convolution_convert_fusion, bf16[512,2560]{1,0:T(8,128)(2,1)S(1)} %convolution_convert_fusion.1, bf16[2560]{0:T(1024)(128)(2,1)S(1)} %get-tuple-element.30), channel_id=2, replica_groups=mesh['dp'=256] {'dp'}, use_global_device_ids=true, to_apply=%region_9.10.clone | all-reduce | flops 3279360 | bytes 19676160
  451.9 1.5 constant_dynamic-slice_fusion.1
  453.5 1.2 constant_dynamic-slice_fusion
  455.9 5.5 %fusion.15 = bf16[384,2560]{1,0:T(8,128)(2,1)} fusion(bf16[384,2560]{1,0:T(8,128)(2,1)} %param.8, bf16[384,2560]{1,0:T(8,128)(2,1)} %param.6, bf16[384,2560]{1,0:T(8,128)(2,1)} %get-tuple-element.54, f32[384]{0:T(512)S(1)} %multiply_multiply_fusion.1, f32[2560]{0:T(1024)S(1)} %convert_element_type.108, f32[384]{0:T(512)S(1)} %copy-done.14), kind=kLoop, calls=%fused_computation.31 | loop fusion | flops 8847360 | bytes 7877632 | tf_op jit(solution)/shard_map/add | solution.py:112
  (69 shorter events, 15.7 us)
Async XLA Ops:
  7.2 123.8 %all-gather.7.cloned.1.call-start = ((), (), s32[]{:S(2)}) async-start(), calls=%async_computation.1 | async-start | bytes 4210688 | tf_op jit(solution)/shard_map/all_gather | solution.py:92
  7.9 240.2 %all-gather.5.cloned.1.call-start = ((), (), s32[]{:S(2)}) async-start(), calls=%async_computation | async-start | bytes 6316032 | tf_op jit(solution)/shard_map/all_gather | solution.py:83
  96.5 0.6 copy-start.10
  97.0 159.3 %copy-start.13 = (f32[384]{0:T(512)}, f32[384]{0:T(512)S(1)}, u32[]{:S(2)}) copy-start(f32[384]{0:T(512)S(1)} %fusion.49) | copy-start | bytes 4612
  97.0 40.1 %copy-start.1 = (bf16[384,2560]{1,0:T(8,128)(2,1)S(1)}, bf16[384,2560]{1,0:T(8,128)(2,1)}, u32[]{:S(2)}) copy-start(bf16[384,2560]{1,0:T(8,128)(2,1)} %param.8) | copy-start | bytes 5898244
  141.0 115.3 %copy-start = (bf16[384,2560]{1,0:T(8,128)(2,1)S(1)}, bf16[384,2560]{1,0:T(8,128)(2,1)}, u32[]{:S(2)}) copy-start(bf16[384,2560]{1,0:T(8,128)(2,1)} %param.6) | copy-start | bytes 5898244
  260.2 1.0 copy-start.4
  263.0 3.8 copy-start.15
  266.5 1.5 copy-start.9
  268.0 1.3 copy-start.5
  268.0 1.3 copy-start.7
  269.4 1.0 copy-start.8
  274.5 1.8 copy-start.12
  274.5 2.1 copy-start.3
  274.5 2.1 copy-start.14
  280.2 4.2 copy-start.6
  284.4 2.6 copy-start.2
  286.9 1.5 copy-start.11
Sparse Core Ops, SparseCore 0:
  11.6 119.3 all-gather.6
  134.8 113.2 all-gather.4
where the time goes:
time: 469 us; the launch traced here: 468 us
  blocking collectives  245 us (52%)
  waiting for transfers between devices  142 us (30%)
  local copies, waits for them, and re-layouts  24.5 us (5%)
  matrix products  23.6 us (5%)
  other arithmetic  18.2 us (4%)
  between operations  14.4 us (3%)
    unnamed x2, blocking collectives  245 us
    all_gather x1, waiting for transfers between devices, per_device(): weight_piece = lax.all_gather(w_qkv, 'dp', axis=0, tiled=True)  107 us
    all_gather x1, waiting for transfers between devices, per_device(): lax.all_gather(w_out, 'dp', axis=1, tiled=True)  33.9 us
    unnamed x40, local copies, waits for them, and re-layouts  21.2 us
  transfers between devices with their start and end apart: 2, of which 2 were waited for; matrix products, arithmetic and copies ran while one was open for 3% of the time, Pallas kernels for 0%

commit v1 on v0

v1 whole, which is shorter than its diff:
```python
import math

import jax
import jax.numpy as jnp
from jax import lax
from jax.experimental import pallas as pl
from jax.experimental.pallas import tpu as pltpu
from jax.sharding import PartitionSpec as P

NY, NZ, NX, NC = 4, 8, 4, 2
D, T, HD = 2560, 384, 128
ROWS = 10
GROUP = NX * NC
BLK = GROUP * ROWS
CH = NZ * BLK
WA_, WB_ = 384, 256
WX = WA_ + WB_
PAD = 16
EPS = 1e-06
LOG_BASE = math.log(1000000.0)
N_COPIES = 256
BF, F32 = jnp.bfloat16, jnp.float32
NT = (((1,), (1,)), ((), ()))
TN = (((0,), (0,)), ((), ()))


def mm(a, b, dims=(((1,), (0,)), ((), ()))):
    return lax.dot_general(a, b, dims, preferred_element_type=F32)


def rms(x):
    return lax.rsqrt(jnp.mean(x * x, axis=-1, keepdims=True) + EPS)


def kernel(
    tok_hbm, go_hbm, seg_ref, gain_ref, wq_ref, wo_ref,
    out_hbm, gt_hbm, s_ref,
    tok, go, sc, scT, goT, rr, blk, xg, tmp, wa, wb, proj, gm, mask, cs, sn,
    qb, kv, pb, mx, dpr, outv, gs,
    ta, sa, ra, ya1, ya2, za, tb, sb, rb, zb, zb4, yb, fin, xs, xr,
    lsem, ssem, rsem,
):
    idx = lax.axis_index("dp")
    me8 = lax.rem(idx, GROUP)
    base = idx - me8
    c = lax.rem(idx, 2)
    o = 1 - c
    x_c = me8
    yz = lax.div(idx, GROUP)
    z = lax.rem(yz, NZ)
    y = lax.div(yz, NZ)

    def ym(k):
        return lax.rem(y + (k + NY), NY)

    def zm(k):
        return lax.rem(z + (k + NZ), NZ)

    def dev(yy, zz):
        return (yy * NZ + zz) * GROUP + x_c

    right_y, left_y = dev(ym(1), z), dev(ym(-1), z)
    right_z, left_z = dev(y, zm(1)), dev(y, zm(-1))
    partner = idx + 1 - 2 * c

    def rows(zz):
        return pl.ds(pl.multiple_of(zz * BLK, 16), BLK)

    copies = []

    def send(src, dst, target):
        n = len(copies)
        copy = pltpu.make_async_remote_copy(
            src_ref=src, dst_ref=dst, send_sem=ssem.at[n], recv_sem=rsem.at[n],
            device_id=(target,), device_id_type=pl.DeviceIdType.MESH,
        )
        copy.start()
        copies.append(copy)
        return copy

    loads = []
    for i, (src, dst) in enumerate(((tok_hbm, tok), (go_hbm, go))):
        for j in range(NY):
            cp = pltpu.make_async_copy(
                src.at[:, pl.ds(j * CH, CH)], dst.at[j], lsem.at[i * NY + j])
            cp.start()
            loads.append(cp)

    barrier = pltpu.get_barrier_semaphore()
    group = [base + lax.rem(me8 + p, GROUP) for p in range(1, GROUP)]
    everyone = group + [right_y, left_y, right_z, left_z]
    for d in everyone:
        pl.semaphore_signal(barrier, inc=1, device_id=(d,), device_id_type=pl.DeviceIdType.MESH)

    diag = lax.broadcasted_iota(jnp.int32, (PAD, ROWS), 0) == lax.broadcasted_iota(
        jnp.int32, (PAD, ROWS), 1)
    gain_diag = jnp.where(diag, jnp.broadcast_to(gain_ref[...].astype(F32), (PAD, ROWS)), 0.0)
    gw = mm(gain_diag.astype(BF), wq_ref[...]).astype(BF)
    wt = mm(diag.astype(F32).astype(BF), wo_ref[...], NT).astype(BF)
    for h in range(NC):
        blk[h, :, :WA_] = gw[:, h * WA_:(h + 1) * WA_]
        blk[h, :, WA_:] = wt[:, h * WB_:(h + 1) * WB_]

    pl.semaphore_wait(barrier, len(everyone))

    xcop = []
    for p in range(1, GROUP):
        t = lax.rem(me8 + p, GROUP)
        xcop.append(send(blk.at[lax.rem(t, 2)], xg.at[me8], base + t))
    xg[me8] = blk[c]

    for j in range(NY):
        loads[j].wait()

    def scale_rows(i, _):
        r0 = pl.ds(pl.multiple_of(i * 16, 16), 16)
        parts = [tok[j, r0, :].astype(F32) for j in range(NY)]
        total = sum(jnp.sum(p * p, axis=-1, keepdims=True) for p in parts)
        r = lax.rsqrt(total * (1.0 / D) + EPS)
        rr[r0, :] = jnp.broadcast_to(r, (16, 128))
        for j in range(NY):
            sc[j, r0, :] = (parts[j] * r).astype(BF)
        return 0

    lax.fori_loop(0, T // 16, scale_rows, 0)

    for cp in xcop:
        cp.wait_recv()
    for i in range(GROUP):
        tmp[i * ROWS:(i + 1) * ROWS, :] = xg[i].astype(F32)[:ROWS, :]
    wa[c, y, rows(z), :] = tmp[:, :WA_].astype(BF)
    wb[c, y, rows(z), :] = tmp[:, WA_:].astype(BF)

    def ablk(yy, zz):
        return wa.at[c, yy, rows(zz), :]

    def bblk(yy, zz):
        return wb.at[c, yy, rows(zz), :]

    def bhalf(h, zz):
        return wb.at[c, pl.ds(2 * h, 2), rows(zz), :]

    offs = [0, -1, 1, -2, 2, -3, 3, -4]
    za_r, za_l, ya_r, ya_l, ya_f, zb_r, zb_l = {}, {}, {}, {}, {}, {}, {}

    def zA(s):
        za_r[s] = send(ablk(y, zm(1 - s)), ablk(y, zm(1 - s)), right_z)
        if s < 4:
            za_l[s] = send(ablk(y, zm(s - 1)), ablk(y, zm(s - 1)), left_z)

    def zA_wait(s):
        za_r[s].wait_recv()
        if s < 4:
            za_l[s].wait_recv()

    def yA(j):
        b = ablk(y, zm(offs[j]))
        ya_r[j] = send(b, b, right_y)
        ya_l[j] = send(b, b, left_y)

    def yA_forward(j):
        ya_r[j].wait_recv()
        ya_l[j].wait_recv()
        if j % 2 == 0:
            b = ablk(ym(-1), zm(offs[j]))
            ya_f[j] = send(b, b, right_y)
        else:
            b = ablk(ym(1), zm(offs[j]))
            ya_f[j] = send(b, b, left_y)

    def zB(s):
        for h in range(2):
            if s < 4 or h == 0:
                b = bhalf(h, zm(1 - s))
                zb_r[s, h] = send(b, b, right_z)
            if s < 4 or h == 1:
                b = bhalf(h, zm(s - 1))
                zb_l[s, h] = send(b, b, left_z)

    def zB_wait(s):
        for h in range(2):
            if s < 4 or h == 0:
                zb_r[s, h].wait_recv()
            if s < 4 or h == 1:
                zb_l[s, h].wait_recv()

    def transpose(src, dst, j):
        for k in range(CH // 128):
            piece = src[j, :, k * 128:(k + 1) * 128].astype(F32)
            dst[j, k * 128:(k + 1) * 128, :] = piece.T.astype(BF)

    zA(1)
    b = bblk(y, z)
    yb1_r = send(b, b, right_y)
    yb1_l = send(b, b, left_y)
    yA(0)

    seg = seg_ref[...].astype(F32)
    row_i = lax.broadcasted_iota(jnp.int32, (T, T), 0)
    col_i = lax.broadcasted_iota(jnp.int32, (T, T), 1)
    seg_s = jnp.broadcast_to(seg, (T, T))
    seg_t = jnp.sum(jnp.where(row_i == col_i, seg_s, 0.0), axis=1, keepdims=True)
    first = jnp.sum(jnp.where(seg_s < seg_t, 1.0, 0.0), axis=1, keepdims=True)
    mask[...] = jnp.where((seg_s == seg_t) & (col_i <= row_i), 1.0, 0.0)
    lane = lax.broadcasted_iota(jnp.int32, (T, HD), 1)
    place = lax.broadcasted_iota(jnp.int32, (T, HD), 0).astype(F32)
    inverse = jnp.exp(lax.rem(lane, HD // 2).astype(F32) * (-2.0 * LOG_BASE / HD))
    angles = (place - first) * inverse
    cs[...] = jnp.cos(angles)
    sn[...] = jnp.where(lane < HD // 2, -1.0, 1.0) * jnp.sin(angles)

    yb1_r.wait_recv()
    yb1_l.wait_recv()
    b = bblk(ym(-1), z)
    yb2 = send(b, b, right_y)
    zA_wait(1)
    zA(2)
    yA(1)
    yA(2)
    transpose(sc, scT, 0)
    yb2.wait_recv()
    zB(1)
    zA_wait(2)
    zA(3)
    yA(3)
    yA(4)
    yA_forward(0)
    transpose(sc, scT, 1)
    zA_wait(3)
    zA(4)
    yA(5)
    yA(6)
    yA_forward(1)
    yA_forward(2)
    transpose(sc, scT, 2)
    zB_wait(1)
    zB(2)
    zA_wait(4)
    yA(7)
    pa_own = send(wa.at[c, y], wa.at[c, y], partner)
    yA_forward(3)
    yA_forward(4)
    transpose(sc, scT, 3)
    zB_wait(2)
    zB(3)
    yA_forward(5)
    yA_forward(6)
    for j in range(NY):
        loads[NY + j].wait()
    transpose(go, goT, 0)
    transpose(go, goT, 1)
    yA_forward(7)
    pa_l = send(wa.at[c, ym(-1)], wa.at[c, ym(-1)], partner)
    pa_r = send(wa.at[c, ym(1)], wa.at[c, ym(1)], partner)
    zB_wait(3)
    zB(4)
    transpose(go, goT, 2)
    transpose(go, goT, 3)

    def project(yy, first_one=False):
        left = sc[yy]
        for h in range(NC):
            part = mm(left, wa[h, yy])
            proj[h] = part if first_one else proj[h] + part

    pa_own.wait_recv()
    project(y, True)
    pa_f = []
    for j in range(4):
        ya_f[j].wait_recv()
        b = ablk(ym(2), zm(offs[j]))
        pa_f.append(send(b, b, partner))
    pa_l.wait_recv()
    project(ym(-1))
    for j in range(4, 8):
        ya_f[j].wait_recv()
        b = ablk(ym(2), zm(offs[j]))
        pa_f.append(send(b, b, partner))
    pa_r.wait_recv()
    project(ym(1))
    zB_wait(4)
    pb_s = [send(wb.at[c, j], wb.at[c, j], partner) for j in range(NY)]
    for cp in pa_f:
        cp.wait_recv()
    project(ym(2))

    def head_cols(h):
        return h // 3, (h % 3) * HD

    def turn(v):
        return v * cs[...] + pltpu.roll(v, HD // 2, 1) * sn[...]

    def unturn(v):
        return v * cs[...] + pltpu.roll(v * sn[...], HD // 2, 1)

    for h in range(5):
        hf, col = head_cols(h)
        v = proj[hf, :, col:col + HD]
        qb[h] = turn(v * rms(v)).astype(BF)
    kv[...] = proj[1, :, 2 * HD:].astype(BF)
    scale = HD ** -0.5
    for h in range(4):
        for i in range(3):
            r0, n = slice(i * 128, (i + 1) * 128), (i + 1) * 128
            s = mm(qb[h, r0, :], qb[4, :n, :], NT) * scale
            w = jnp.exp(s) * mask[r0, :n]
            p = (w / jnp.sum(w, axis=-1, keepdims=True)).astype(BF)
            pb[h, r0, :n] = p
            mx[h // 2, r0, (h % 2) * HD:(h % 2 + 1) * HD] = mm(p, kv[:n, :]).astype(BF)

    rb_s = []
    for j in range(NY):
        sb[j] = mm(goT[j], mx[o]).astype(BF)
        rb_s.append(send(sb.at[j], rb.at[j], partner))
    for j in range(NY):
        tb[j] = mm(goT[j], mx[c]).astype(BF)
    for cp in pb_s:
        cp.wait_recv()
    for h in range(NC):
        gm[h] = sum(mm(go[j], wb[h, j]) for j in range(NY)).astype(BF)
    for j in range(NY):
        rb_s[j].wait_recv()
        tb[j] = (tb[j].astype(F32) + rb[j].astype(F32)).astype(BF)

    def tbz(zz, h0=0, n=NY):
        return tb.at[pl.ds(h0, n), rows(zz), :]

    def add_into(ref, *others):
        total = ref[...].astype(F32)
        for other in others:
            total = total + other[...].astype(F32)
        ref[...] = total.astype(BF)

    b4r = send(tbz(zm(4), 0, 2), zb4.at[0], right_z)
    b4l = send(tbz(zm(-4), 2, 2), zb4.at[1], left_z)
    bz = {}

    def zB_rs(s):
        if s == 3:
            b4r.wait_recv()
            add_into(tbz(zm(3), 0, 2), zb4.at[0])
            b4l.wait_recv()
            add_into(tbz(zm(-3), 2, 2), zb4.at[1])
        else:
            for side, k in ((0, s), (1, -s)):
                bz[side, s + 1].wait_recv()
                add_into(tbz(zm(k)), zb.at[side, s])
        bz[0, s] = send(tbz(zm(s)), zb.at[0, s - 1], right_z)
        bz[1, s] = send(tbz(zm(-s)), zb.at[1, s - 1], left_z)

    def head_back(h, dk, dv):
        dq = []
        for i in range(3):
            r0, n = slice(i * 128, (i + 1) * 128), (i + 1) * 128
            do = gm[h // 2, r0, (h % 2) * HD:(h % 2 + 1) * HD]
            dp = mm(do, kv[:n, :], NT)
            p = pb[h, r0, :n]
            pf = p.astype(F32)
            delta = jnp.sum(pf * dp, axis=-1, keepdims=True)
            ds = (pf * (dp - delta) * scale).astype(BF)
            dq.append(mm(ds, qb[4, :n, :]))
            tk = mm(ds, qb[h, r0, :], TN)
            tv = mm(p, do, TN)
            for m in range(i + 1):
                dk[m] = dk[m] + tk[m * 128:(m + 1) * 128]
                dv[m] = dv[m] + tv[m * 128:(m + 1) * 128]
        return jnp.concatenate(dq, axis=0)

    def project_back(h, d):
        hf, col = head_cols(h)
        v = proj[hf, :, col:col + HD]
        r = rms(v)
        xn = v * r
        dn = unturn(d)
        grad = r * (dn - xn * jnp.mean(dn * xn, axis=-1, keepdims=True))
        dpr[hf, :, col:col + HD] = grad.astype(BF)

    dk = [jnp.zeros((128, HD), F32)] * 3
    dv = [jnp.zeros((128, HD), F32)] * 3
    for h in range(4):
        project_back(h, head_back(h, dk, dv))
        if h < 3:
            zB_rs(3 - h)
    project_back(4, jnp.concatenate(dk, axis=0))
    dpr[1, :, 2 * HD:] = jnp.concatenate(dv, axis=0).astype(BF)

    ra_s = {}
    for k in (2, 1, 3, 0):
        yy = ym(k)
        sa[yy] = mm(scT[yy], dpr[o]).astype(BF)
        ra_s[k] = send(sa.at[yy], ra.at[yy], partner)
        ta[yy] = mm(scT[yy], dpr[c]).astype(BF)

    bz[0, 1].wait_recv()
    bz[1, 1].wait_recv()
    add_into(tbz(z), zb.at[0, 0], zb.at[1, 0])
    yb_r2 = send(tb.at[ym(2), rows(z), :], yb.at[0], right_y)
    yb_l = send(tb.at[ym(-1), rows(z), :], yb.at[1], left_y)

    roffs = [4, 3, -3, 2, -2, 1, -1, 0]

    def tblk(yy, j):
        return ta.at[yy, rows(zm(roffs[j])), :]

    s1, s2r, s2l, sz = {}, {}, {}, {}
    ra_s[2].wait_recv()
    for j in range(8):
        add_into(tblk(ym(2), j), ra.at[ym(2), rows(zm(roffs[j])), :])
        s1[j] = send(tblk(ym(2), j), ya1.at[j], right_y if j % 2 == 0 else left_y)
    ra_s[1].wait_recv()
    add_into(ta.at[ym(1)], ra.at[ym(1)])
    ra_s[3].wait_recv()
    add_into(ta.at[ym(3)], ra.at[ym(3)])

    yb_r2.wait_recv()
    add_into(tb.at[ym(1), rows(z), :], yb.at[0])
    yb_r1 = send(tb.at[ym(1), rows(z), :], yb.at[2], right_y)

    def step2(j):
        s1[j].wait_recv()
        add_into(tblk(ym(1) if j % 2 == 0 else ym(3), j), ya1.at[j])
        s2r[j] = send(tblk(ym(1), j), ya2.at[0, j], right_y)
        s2l[j] = send(tblk(ym(3), j), ya2.at[1, j], left_y)

    def step3(j):
        s2r[j].wait_recv()
        s2l[j].wait_recv()
        add_into(tblk(y, j), ya2.at[0, j], ya2.at[1, j])

    def step_z(j):
        if j == 0:
            sz[0] = send(tblk(y, 0), za.at[0], right_z)
        elif j == 7:
            return
        elif j % 2 == 1:
            n = (j + 1) // 2
            sz[n - 1].wait_recv()
            add_into(tblk(y, j), za.at[n - 1])
            sz[n] = send(tblk(y, j), za.at[n], right_z)
        else:
            n = 3 + j // 2
            if n > 4:
                sz[n - 1].wait_recv()
                add_into(tblk(y, j), za.at[n - 1])
            sz[n] = send(tblk(y, j), za.at[n], left_z)

    def out_chunk(j):
        update = sum(mm(mx[h], wb[h, j], NT) for h in range(NC))
        outv[j] = (tok[j].astype(F32) + update).astype(BF)

    def gs_chunk(j):
        gs[j] = sum(mm(dpr[h], wa[h, j], NT) for h in range(NC))

    for j in range(4):
        step2(j)
        out_chunk(j)
    stores = []
    for j in range(NY):
        cp = pltpu.make_async_copy(
            outv.at[j], out_hbm.at[:, pl.ds(j * CH, CH)], lsem.at[2 * NY + j])
        cp.start()
        stores.append(cp)
    ra_s[0].wait_recv()
    add_into(ta.at[y], ra.at[y])
    step2(4)
    step2(5)
    gs_chunk(0)
    step3(0)
    step_z(0)
    step2(6)
    step2(7)
    gs_chunk(1)
    step3(1)
    step3(2)
    step_z(1)
    step_z(2)
    gs_chunk(2)
    step3(3)
    step3(4)
    step_z(3)
    step_z(4)
    gs_chunk(3)
    step3(5)
    step3(6)
    step_z(5)
    step_z(6)

    def token_rows(i, _):
        r0 = pl.ds(pl.multiple_of(i * 16, 16), 16)
        r = rr[r0, :][:, :1]
        xn = [tok[j, r0, :].astype(F32) * r for j in range(NY)]
        g = [gs[j, r0, :] for j in range(NY)]
        dot = sum(jnp.sum(a * b, axis=-1, keepdims=True) for a, b in zip(xn, g)) * (1.0 / D)
        for j in range(NY):
            path = (r * (g[j] - xn[j] * dot)).astype(BF).astype(F32)
            go[j, r0, :] = (go[j, r0, :].astype(F32) + path).astype(BF)
        return 0

    lax.fori_loop(0, T // 16, token_rows, 0)
    for j in range(NY):
        cp = pltpu.make_async_copy(
            go.at[j], gt_hbm.at[:, pl.ds(j * CH, CH)], lsem.at[3 * NY + j])
        cp.start()
        stores.append(cp)

    step3(7)
    sz[3].wait_recv()
    sz[6].wait_recv()
    fin[:BLK, :WA_] = (
        tblk(y, 7)[...].astype(F32) + za[3].astype(F32) + za[6].astype(F32))
    yb_r1.wait_recv()
    yb_l.wait_recv()
    fin[:BLK, WA_:] = (
        tb[y, rows(z), :].astype(F32) + yb[1].astype(F32) + yb[2].astype(F32))
    fin[BLK:, :] = jnp.zeros((PAD, WX), F32)

    for i in range(GROUP):
        xs[i] = fin[i * ROWS:i * ROWS + PAD, :].astype(BF)
    last = []
    for p in range(1, GROUP):
        t = lax.rem(me8 + p, GROUP)
        last.append(send(xs.at[t], xr.at[me8], base + t))
    xr[me8] = xs[me8]
    for cp in last:
        cp.wait_recv()
    for h in range(NC):
        s_ref[h] = sum(xr[2 * i + h].astype(F32) for i in range(NX))

    for cp in copies:
        cp.wait_send()
    for cp in stores:
        cp.wait()


def block_step(tokens, segment_ids, grad_out, norm_gain, w_qkv, w_out):
    any_, vm = pl.BlockSpec(memory_space=pl.ANY), pl.BlockSpec(memory_space=pltpu.VMEM)
    v = pltpu.VMEM
    out, grad_tokens, sums = pl.pallas_call(
        kernel,
        out_shape=(
            jax.ShapeDtypeStruct((T, D), BF),
            jax.ShapeDtypeStruct((T, D), BF),
            jax.ShapeDtypeStruct((NC, PAD, WX), F32),
        ),
        in_specs=[any_, any_, vm, vm, vm, vm],
        out_specs=(any_, any_, vm),
        scratch_shapes=[
            v((NY, T, CH), BF), v((NY, T, CH), BF), v((NY, T, CH), BF),
            v((NY, CH, T), BF), v((NY, CH, T), BF), v((T, 128), F32),
            v((NC, PAD, WX), BF), v((GROUP, PAD, WX), BF), v((BLK, WX), F32),
            v((NC, NY, CH, WA_), BF), v((NC, NY, CH, WB_), BF),
            v((NC, T, WA_), F32), v((NC, T, WB_), BF), v((T, T), F32),
            v((T, HD), F32), v((T, HD), F32),
            v((5, T, HD), BF), v((T, HD), BF), v((4, T, T), BF),
            v((NC, T, WB_), BF), v((NC, T, WA_), BF), v((NY, T, CH), BF), v((NY, T, CH), F32),
            v((NY, CH, WA_), BF), v((NY, CH, WA_), BF), v((NY, CH, WA_), BF),
            v((NZ, BLK, WA_), BF), v((2, NZ, BLK, WA_), BF), v((7, BLK, WA_), BF),
            v((NY, CH, WB_), BF), v((NY, CH, WB_), BF), v((NY, CH, WB_), BF),
            v((2, 3, NY, BLK, WB_), BF), v((2, 2, BLK, WB_), BF), v((3, BLK, WB_), BF),
            v((BLK + PAD, WX), F32), v((GROUP, PAD, WX), BF), v((GROUP, PAD, WX), BF),
            pltpu.SemaphoreType.DMA((4 * NY,)),
            pltpu.SemaphoreType.DMA((N_COPIES,)), pltpu.SemaphoreType.DMA((N_COPIES,)),
        ],
        compiler_params=pltpu.CompilerParams(
            collective_id=0, has_side_effects=True, vmem_limit_bytes=60 * 2 ** 20),
        name="block_step",
    )(tokens, grad_out, segment_ids, norm_gain.reshape(1, ROWS), w_qkv, w_out)
    scaled_sum = jnp.concatenate([sums[0, :ROWS, :WA_], sums[1, :ROWS, :WA_]], axis=1)
    out_sum = jnp.concatenate([sums[0, :ROWS, WA_:], sums[1, :ROWS, WA_:]], axis=1)
    grad_qkv = scaled_sum * norm_gain.astype(F32)[:, None]
    grad_gain = jnp.sum(scaled_sum * w_qkv.astype(F32), axis=1)
    return out, grad_tokens, grad_qkv, out_sum.T, grad_gain


def solution(mesh):
    return jax.shard_map(
        block_step,
        mesh=mesh,
        in_specs=(P("dp", None), P("dp", None), P("dp", None), P("dp"), P("dp", None),
                  P(None, "dp")),
        out_specs=(P("dp", None), P("dp", None), P("dp", None), P(None, "dp"), P("dp")),
        check_vma=False,
    )
```

time: 469 us -> 122 us (0.26)
  blocking collectives: 245 us -> 0 us
  waiting for transfers between devices: 142 us -> 0 us
  Pallas kernels: 0 us -> 111 us
  matrix products: 23.6 us -> 0 us
  local copies, waits for them, and re-layouts: 24.5 us -> 7.37 us
  other arithmetic: 18.2 us -> 1.94 us
  between operations: 14.4 us -> 0.66 us
    unnamed x2 -> x0, blocking collectives: 245 us -> none
    all_gather x2 -> x0, waiting for transfers between devices: 141 us -> none  [the longest x1 107 us: per_device(): weight_piece = lax.all_gather(w_qkv, 'dp', axis=0, tiled=True)]
    pallas_call x0 -> x1, Pallas kernels: none -> 111 us  [block_step(): pl.pallas_call(kernel, out_shape=(jax.ShapeDtypeStruct((T, D), BF), jax.S...]
    dot_general x12 -> x0, matrix products: 23.6 us -> none  [the longest x2 7.75 us: section_attention(): projected = jnp.dot(normed, w_qkv, preferred_element_type=jnp.float32)]
    unnamed x40 -> x9, local copies, waits for them, and re-layouts: 21.2 us -> 5.87 us
    add x1 -> x0, other arithmetic: 5.49 us -> none  [per_device(): grad_residual + grad_normpath]
  transfers between devices with their start and end apart: 2 -> 0, of which waited for: 2 -> 0; matrix products, arithmetic and copies ran while one was open for 3% -> 0% of each run, Pallas kernels for 0% -> 0%
where the time goes in v1:
time: 122 us; the launch traced here: 121 us
  Pallas kernels  111 us (91%)
  local copies, waits for them, and re-layouts  7.37 us (6%)
  other arithmetic  1.94 us (2%)
    pallas_call x1, Pallas kernels, block_step(): pl.pallas_call(kernel, out_shape=(jax.ShapeDtypeStruct((T, D), BF), jax.S...  111 us
    unnamed x9, local copies, waits for them, and re-layouts  5.87 us

profile of v1, /device:TPU:1, one launch (start us, length us, event | category | flops | bytes accessed | tf_op | source)
XLA Modules:
  0.0 121.3 jit_solution(2900033497879943265)
XLA Ops:
  0.6 1.5 %copy.11.wo_ref = bf16[512,10]{1,0:T(8,128)(2,1)} copy(bf16[512,10]{0,1:T(8,128)(2,1)} %param.11) | data formatting | bytes 20480 | tf_op args[5]
  2.1 0.0 copy-start.2
  2.1 0.0 copy-start.1
  2.1 111.3 %block_step.1 = (bf16[384,2560]{1,0:T(8,128)(2,1)}, bf16[384,2560]{1,0:T(8,128)(2,1)}, f32[2,16,640]{2,1,0:T(8,128)}) custom-call(bf16[384,2560]{1,0:T(8,128)(2,1)} %tok_hbm.1, bf16[384,2560]{1,0:T(8,128)(2,1)} %go_hbm.1, s32[1,384]{1,0:T(1,128)} %seg_ref.1, bf16[1,10]{1,0:T(2,128)(2,1)} %bitcast.11, bf16[10,768]{1,0:T(8,128)(2,1)} %wq_ref.1, ...), custom_call_target="tpu_custom_call" | custom-call | tf_op jit(solution)/shard_map/block_step/pallas_call | solution.py:538
  113.4 0.8 slice_bitcast_fusion.1
  114.2 0.0 copy-done.2
  114.2 0.0 copy-done.1
  114.2 1.3 %multiply_reduce_fusion = (f32[10]{0:T(128)}, f32[10,768]{1,0:T(8,128)}) fusion(bf16[10,768]{1,0:T(8,128)(2,1)S(1)} %copy-done.1, f32[10,384]{1,0:T(8,128)S(1)} %get-tuple-element.14, f32[10,384]{1,0:T(8,128)S(1)} %get-tuple-element.13, f32[10]{0:T(128)S(1)} %convert_element_type.6), kind=kLoop, calls=%fused_computation.1 | loop fusion | flops 38390 | bytes 76880 | tf_op jit(solution)/shard_map/reduce_sum | solution.py:571
  115.5 0.7 slice_bitcast_fusion.3
  116.3 0.6 maximum_bitcast_fusion
  116.9 0.0 copy-start
  116.9 3.1 %copy.14 = bf16[384,2560]{1,0:T(8,128)(2,1)} copy(bf16[384,2560]{1,0:T(8,128)(2,1)} %get-tuple-element.22) | data formatting | bytes 3932160
  120.0 0.0 copy-done
  120.0 1.3 %copy.15 = bf16[384,2560]{1,0:T(8,128)(2,1)} copy(bf16[384,2560]{1,0:T(8,128)(2,1)S(1)} %copy-done) | data formatting | bytes 3932160
  (1 shorter events, 0.0 us)
Async XLA Ops:
  2.1 112.1 %copy-start.2 = (bf16[10]{0:T(256)(128)(2,1)S(1)}, bf16[10]{0:T(256)(128)(2,1)}, u32[]{:S(2)}) copy-start(bf16[10]{0:T(256)(128)(2,1)} %param.9) | copy-start | bytes 64
  2.1 112.1 %copy-start.1 = (bf16[10,768]{1,0:T(8,128)(2,1)S(1)}, bf16[10,768]{1,0:T(8,128)(2,1)}, u32[]{:S(2)}) copy-start(bf16[10,768]{1,0:T(8,128)(2,1)} %wq_ref.1) | copy-start | bytes 46084
  116.9 3.1 %copy-start = (bf16[384,2560]{1,0:T(8,128)(2,1)S(1)}, bf16[384,2560]{1,0:T(8,128)(2,1)}, u32[]{:S(2)}) copy-start(bf16[384,2560]{1,0:T(8,128)(2,1)} %get-tuple-element.23) | copy-start | bytes 5898244

commit v2 on v1

--- a/solution.py
+++ b/solution.py
@@ -34,18 +34,18 @@
 
 def kernel(
     tok_hbm, go_hbm, seg_ref, gain_ref, wq_ref, wo_ref,
-    out_hbm, gt_hbm, s_ref,
+    out_ref, gt_ref, s_ref,
     tok, go, sc, scT, goT, rr, blk, xg, tmp, wa, wb, proj, gm, mask, cs, sn,
-    qb, kv, pb, mx, dpr, outv, gs,
-    ta, sa, ra, ya1, ya2, za, tb, sb, rb, zb, zb4, yb, fin, xs, xr,
-    lsem, ssem, rsem,
+    qb, kv, pb, mx, dpr, gs,
+    ta, sa, ra, ya1, ya2, za, tb, sb, rb, xb, zb, fin, finb, xs, xr, xsb, xrb,
+    lsem, ssem, rsem, fsem,
 ):
     idx = lax.axis_index("dp")
     me8 = lax.rem(idx, GROUP)
     base = idx - me8
     c = lax.rem(idx, 2)
     o = 1 - c
-    x_c = me8
+    xi = lax.div(me8, 2)
     yz = lax.div(idx, GROUP)
     z = lax.rem(yz, NZ)
     y = lax.div(yz, NZ)
@@ -57,7 +57,10 @@
         return lax.rem(z + (k + NZ), NZ)
 
     def dev(yy, zz):
-        return (yy * NZ + zz) * GROUP + x_c
+        return (yy * NZ + zz) * GROUP + me8
+
+    def xdev(k):
+        return base + lax.rem(me8 + 2 * k, GROUP)
 
     right_y, left_y = dev(ym(1), z), dev(ym(-1), z)
     right_z, left_z = dev(y, zm(1)), dev(y, zm(-1))
@@ -78,6 +81,25 @@
         copies.append(copy)
         return copy
 
+    barrier = pltpu.get_barrier_semaphore()
+
+    def greet(d):
+        pl.semaphore_signal(barrier, inc=1, device_id=(d,), device_id_type=pl.DeviceIdType.MESH)
+
+    greetings = [base + lax.rem(me8 + p, GROUP) for p in range(1, GROUP)]
+    greetings += [dev(ym(k), z) for k in range(1, NY)]
+    greetings += [dev(y, zm(k)) for k in range(1, NZ)]
+    for k in range(NY):
+        for core in (c, o):
+            if k > 0 or core is o:
+                greetings.append((ym(k) * NZ + z) * GROUP + 2 * y + core)
+    for d in greetings:
+        greet(d)
+
+    @pl.when(y != xi)
+    def _():
+        greet((y * NZ + z) * GROUP + 2 * y + c)
+
     loads = []
     for i, (src, dst) in enumerate(((tok_hbm, tok), (go_hbm, go))):
         for j in range(NY):
@@ -86,22 +108,16 @@
             cp.start()
             loads.append(cp)
 
-    barrier = pltpu.get_barrier_semaphore()
-    group = [base + lax.rem(me8 + p, GROUP) for p in range(1, GROUP)]
-    everyone = group + [right_y, left_y, right_z, left_z]
-    for d in everyone:
-        pl.semaphore_signal(barrier, inc=1, device_id=(d,), device_id_type=pl.DeviceIdType.MESH)
-
     diag = lax.broadcasted_iota(jnp.int32, (PAD, ROWS), 0) == lax.broadcasted_iota(
         jnp.int32, (PAD, ROWS), 1)
     gain_diag = jnp.where(diag, jnp.broadcast_to(gain_ref[...].astype(F32), (PAD, ROWS)), 0.0)
     gw = mm(gain_diag.astype(BF), wq_ref[...]).astype(BF)
-    wt = mm(diag.astype(F32).astype(BF), wo_ref[...], NT).astype(BF)
+    wt = mm(diag.astype(F32).astype(BF), wo_ref[...]).astype(BF)
     for h in range(NC):
         blk[h, :, :WA_] = gw[:, h * WA_:(h + 1) * WA_]
         blk[h, :, WA_:] = wt[:, h * WB_:(h + 1) * WB_]
 
-    pl.semaphore_wait(barrier, len(everyone))
+    pl.semaphore_wait(barrier, jnp.where(y == xi, len(greetings), len(greetings) + 1))
 
     xcop = []
     for p in range(1, GROUP):
@@ -122,7 +138,7 @@
             sc[j, r0, :] = (parts[j] * r).astype(BF)
         return 0
 
-    lax.fori_loop(0, T // 16, scale_rows, 0)
+    lax.fori_loop(0, T // 16, scale_rows, 0, unroll=2)
 
     for cp in xcop:
         cp.wait_recv()
@@ -137,11 +153,8 @@
     def bblk(yy, zz):
         return wb.at[c, yy, rows(zz), :]
 
-    def bhalf(h, zz):
-        return wb.at[c, pl.ds(2 * h, 2), rows(zz), :]
-
     offs = [0, -1, 1, -2, 2, -3, 3, -4]
-    za_r, za_l, ya_r, ya_l, ya_f, zb_r, zb_l = {}, {}, {}, {}, {}, {}, {}
+    za_r, za_l, ya_r, ya_l, ya_f, zb_c, xb_c = {}, {}, {}, {}, {}, {}, []
 
     def zA(s):
         za_r[s] = send(ablk(y, zm(1 - s)), ablk(y, zm(1 - s)), right_z)
@@ -168,21 +181,15 @@
             b = ablk(ym(1), zm(offs[j]))
             ya_f[j] = send(b, b, left_y)
 
-    def zB(s):
-        for h in range(2):
-            if s < 4 or h == 0:
-                b = bhalf(h, zm(1 - s))
-                zb_r[s, h] = send(b, b, right_z)
-            if s < 4 or h == 1:
-                b = bhalf(h, zm(s - 1))
-                zb_l[s, h] = send(b, b, left_z)
-
-    def zB_wait(s):
-        for h in range(2):
-            if s < 4 or h == 0:
-                zb_r[s, h].wait_recv()
-            if s < 4 or h == 1:
-                zb_l[s, h].wait_recv()
+    def zB(k):
+        b = bblk(xi, z)
+        zb_c[k] = send(b, b, dev(y, zm(k)))
+
+    def xB(k):
+        zb_c[k].wait_recv()
+        b = bblk(xi, zm(-k))
+        for m in (1, 3, 2):
+            xb_c.append(send(b, b, xdev(m)))
 
     def transpose(src, dst, j):
         for k in range(CH // 128):
@@ -191,8 +198,7 @@
 
     zA(1)
     b = bblk(y, z)
-    yb1_r = send(b, b, right_y)
-    yb1_l = send(b, b, left_y)
+    yb_c = [send(b, b, dev(ym(k), z)) for k in (1, 3, 2)]
     yA(0)
 
     seg = seg_ref[...].astype(F32)
@@ -209,53 +215,50 @@
     cs[...] = jnp.cos(angles)
     sn[...] = jnp.where(lane < HD // 2, -1.0, 1.0) * jnp.sin(angles)
 
-    yb1_r.wait_recv()
-    yb1_l.wait_recv()
-    b = bblk(ym(-1), z)
-    yb2 = send(b, b, right_y)
+    for cp in yb_c:
+        cp.wait_recv()
     zA_wait(1)
     zA(2)
     yA(1)
     yA(2)
+    for k in (1, 7, 2, 6, 3, 5, 4):
+        zB(k)
     transpose(sc, scT, 0)
-    yb2.wait_recv()
-    zB(1)
+    yA_forward(0)
     zA_wait(2)
     zA(3)
     yA(3)
     yA(4)
-    yA_forward(0)
     transpose(sc, scT, 1)
+    yA_forward(1)
+    yA_forward(2)
     zA_wait(3)
     zA(4)
     yA(5)
     yA(6)
-    yA_forward(1)
-    yA_forward(2)
+    xB(1)
+    xB(7)
     transpose(sc, scT, 2)
-    zB_wait(1)
-    zB(2)
+    yA_forward(3)
+    yA_forward(4)
     zA_wait(4)
     yA(7)
     pa_own = send(wa.at[c, y], wa.at[c, y], partner)
-    yA_forward(3)
-    yA_forward(4)
+    xB(2)
+    xB(6)
     transpose(sc, scT, 3)
-    zB_wait(2)
-    zB(3)
     yA_forward(5)
     yA_forward(6)
     for j in range(NY):
         loads[NY + j].wait()
-    transpose(go, goT, 0)
-    transpose(go, goT, 1)
+    xB(3)
+    xB(5)
+    xB(4)
     yA_forward(7)
     pa_l = send(wa.at[c, ym(-1)], wa.at[c, ym(-1)], partner)
     pa_r = send(wa.at[c, ym(1)], wa.at[c, ym(1)], partner)
-    zB_wait(3)
-    zB(4)
-    transpose(go, goT, 2)
-    transpose(go, goT, 3)
+    for j in range(NY):
+        transpose(go, goT, j)
 
     def project(yy, first_one=False):
         left = sc[yy]
@@ -278,8 +281,6 @@
         pa_f.append(send(b, b, partner))
     pa_r.wait_recv()
     project(ym(1))
-    zB_wait(4)
-    pb_s = [send(wb.at[c, j], wb.at[c, j], partner) for j in range(NY)]
     for cp in pa_f:
         cp.wait_recv()
     project(ym(2))
@@ -307,6 +308,10 @@
             p = (w / jnp.sum(w, axis=-1, keepdims=True)).astype(BF)
             pb[h, r0, :n] = p
             mx[h // 2, r0, (h % 2) * HD:(h % 2 + 1) * HD] = mm(p, kv[:n, :]).astype(BF)
+        if h == 1:
+            for cp in xb_c:
+                cp.wait_recv()
+            pb_s = [send(wb.at[c, j], wb.at[c, j], partner) for j in range(NY)]
 
     rb_s = []
     for j in range(NY):
@@ -322,31 +327,16 @@
         rb_s[j].wait_recv()
         tb[j] = (tb[j].astype(F32) + rb[j].astype(F32)).astype(BF)
 
-    def tbz(zz, h0=0, n=NY):
-        return tb.at[pl.ds(h0, n), rows(zz), :]
+    xb_s = []
+    for m in (1, 3, 2):
+        t = lax.rem(xi + m, NX)
+        xb_s.append(send(tb.at[t], xb.at[m - 1], xdev(m)))
 
     def add_into(ref, *others):
         total = ref[...].astype(F32)
         for other in others:
             total = total + other[...].astype(F32)
         ref[...] = total.astype(BF)
-
-    b4r = send(tbz(zm(4), 0, 2), zb4.at[0], right_z)
-    b4l = send(tbz(zm(-4), 2, 2), zb4.at[1], left_z)
-    bz = {}
-
-    def zB_rs(s):
-        if s == 3:
-            b4r.wait_recv()
-            add_into(tbz(zm(3), 0, 2), zb4.at[0])
-            b4l.wait_recv()
-            add_into(tbz(zm(-3), 2, 2), zb4.at[1])
-        else:
-            for side, k in ((0, s), (1, -s)):
-                bz[side, s + 1].wait_recv()
-                add_into(tbz(zm(k)), zb.at[side, s])
-        bz[0, s] = send(tbz(zm(s)), zb.at[0, s - 1], right_z)
-        bz[1, s] = send(tbz(zm(-s)), zb.at[1, s - 1], left_z)
 
     def head_back(h, dk, dv):
         dq = []
@@ -379,8 +369,6 @@
     dv = [jnp.zeros((128, HD), F32)] * 3
     for h in range(4):
         project_back(h, head_back(h, dk, dv))
-        if h < 3:
-            zB_rs(3 - h)
     project_back(4, jnp.concatenate(dk, axis=0))
     dpr[1, :, 2 * HD:] = jnp.concatenate(dv, axis=0).astype(BF)
 
@@ -390,12 +378,6 @@
         sa[yy] = mm(scT[yy], dpr[o]).astype(BF)
         ra_s[k] = send(sa.at[yy], ra.at[yy], partner)
         ta[yy] = mm(scT[yy], dpr[c]).astype(BF)
-
-    bz[0, 1].wait_recv()
-    bz[1, 1].wait_recv()
-    add_into(tbz(z), zb.at[0, 0], zb.at[1, 0])
-    yb_r2 = send(tb.at[ym(2), rows(z), :], yb.at[0], right_y)
-    yb_l = send(tb.at[ym(-1), rows(z), :], yb.at[1], left_y)
 
     roffs = [4, 3, -3, 2, -2, 1, -1, 0]
 
@@ -411,10 +393,6 @@
     add_into(ta.at[ym(1)], ra.at[ym(1)])
     ra_s[3].wait_recv()
     add_into(ta.at[ym(3)], ra.at[ym(3)])
-
-    yb_r2.wait_recv()
-    add_into(tb.at[ym(1), rows(z), :], yb.at[0])
-    yb_r1 = send(tb.at[ym(1), rows(z), :], yb.at[2], right_y)
 
     def step2(j):
         s1[j].wait_recv()
@@ -446,20 +424,60 @@
 
     def out_chunk(j):
         update = sum(mm(mx[h], wb[h, j], NT) for h in range(NC))
-        outv[j] = (tok[j].astype(F32) + update).astype(BF)
+        out_ref[:, j * CH:(j + 1) * CH] = (tok[j].astype(F32) + update).astype(BF)
 
     def gs_chunk(j):
         gs[j] = sum(mm(dpr[h], wa[h, j], NT) for h in range(NC))
 
-    for j in range(4):
-        step2(j)
-        out_chunk(j)
-    stores = []
-    for j in range(NY):
-        cp = pltpu.make_async_copy(
-            outv.at[j], out_hbm.at[:, pl.ds(j * CH, CH)], lsem.at[2 * NY + j])
-        cp.start()
-        stores.append(cp)
+    zb_s = []
+
+    def sum_x():
+        for cp in xb_s:
+            cp.wait_recv()
+        add_into(tb.at[xi], xb.at[0], xb.at[1], xb.at[2])
+        for k in (4, 3, 5, 2, 6, 1, 7):
+            zb_s.append(send(tb.at[xi, rows(zm(k)), :], zb.at[k - 1], dev(y, zm(k))))
+
+    def piece_copy(p):
+        t = lax.rem(me8 + p, GROUP)
+        return pltpu.make_async_remote_copy(
+            src_ref=xsb.at[t], dst_ref=xrb.at[2 * y + c],
+            send_sem=fsem.at[p], recv_sem=fsem.at[GROUP + 2 * y + c],
+            device_id=((xi * NZ + z) * GROUP + t,), device_id_type=pl.DeviceIdType.MESH,
+        )
+
+    def self_copy():
+        return pltpu.make_async_copy(
+            xsb.at[me8], xrb.at[2 * y + c], fsem.at[GROUP + 2 * y + c])
+
+    def sum_z():
+        for cp in zb_s:
+            cp.wait_recv()
+        finb[:BLK, :] = tb[xi, rows(z), :].astype(F32) + sum(
+            zb[k].astype(F32) for k in range(NZ - 1))
+        finb[BLK:, :] = jnp.zeros((PAD, WB_), F32)
+        for i in range(GROUP):
+            xsb[i] = finb[i * ROWS:i * ROWS + PAD, :].astype(BF)
+        for p in range(1, GROUP):
+            piece_copy(p).start()
+
+        @pl.when(y != xi)
+        def _():
+            piece_copy(0).start()
+
+        @pl.when(y == xi)
+        def _():
+            self_copy().start()
+
+    step2(0)
+    out_chunk(0)
+    step2(1)
+    out_chunk(1)
+    step2(2)
+    out_chunk(2)
+    sum_x()
+    step2(3)
+    out_chunk(3)
     ra_s[0].wait_recv()
     add_into(ta.at[y], ra.at[y])
     step2(4)
@@ -493,26 +511,17 @@
         dot = sum(jnp.sum(a * b, axis=-1, keepdims=True) for a, b in zip(xn, g)) * (1.0 / D)
         for j in range(NY):
             path = (r * (g[j] - xn[j] * dot)).astype(BF).astype(F32)
-            go[j, r0, :] = (go[j, r0, :].astype(F32) + path).astype(BF)
+            gt_ref[r0, j * CH:(j + 1) * CH] = (go[j, r0, :].astype(F32) + path).astype(BF)
         return 0
 
-    lax.fori_loop(0, T // 16, token_rows, 0)
-    for j in range(NY):
-        cp = pltpu.make_async_copy(
-            go.at[j], gt_hbm.at[:, pl.ds(j * CH, CH)], lsem.at[3 * NY + j])
-        cp.start()
-        stores.append(cp)
-
+    lax.fori_loop(0, T // 16, token_rows, 0, unroll=2)
+    sum_z()
     step3(7)
     sz[3].wait_recv()
     sz[6].wait_recv()
-    fin[:BLK, :WA_] = (
+    fin[:BLK, :] = (
         tblk(y, 7)[...].astype(F32) + za[3].astype(F32) + za[6].astype(F32))
-    yb_r1.wait_recv()
-    yb_l.wait_recv()
-    fin[:BLK, WA_:] = (
-        tb[y, rows(z), :].astype(F32) + yb[1].astype(F32) + yb[2].astype(F32))
-    fin[BLK:, :] = jnp.zeros((PAD, WX), F32)
+    fin[BLK:, :] = jnp.zeros((PAD, WA_), F32)
 
     for i in range(GROUP):
         xs[i] = fin[i * ROWS:i * ROWS + PAD, :].astype(BF)
@@ -521,29 +530,66 @@
         t = lax.rem(me8 + p, GROUP)
         last.append(send(xs.at[t], xr.at[me8], base + t))
     xr[me8] = xs[me8]
+    for i in range(GROUP):
+        pltpu.make_async_copy(xsb.at[i], xrb.at[i], fsem.at[GROUP + i]).wait()
+    for h in range(NC):
+        s_ref[h, :, WA_:] = sum(xrb[2 * i + h].astype(F32) for i in range(NY))
+    for cp in copies[:-len(last)]:
+        cp.wait_send()
+    for p in range(1, GROUP):
+        piece_copy(p).wait_send()
+
+    @pl.when(y != xi)
+    def _():
+        piece_copy(0).wait_send()
+
     for cp in last:
         cp.wait_recv()
     for h in range(NC):
-        s_ref[h] = sum(xr[2 * i + h].astype(F32) for i in range(NX))
-
-    for cp in copies:
+        s_ref[h, :, :WA_] = sum(xr[2 * i + h].astype(F32) for i in range(NX))
+    for cp in last:
         cp.wait_send()
-    for cp in stores:
+
+
+def finish_kernel(out_in, gt_in, s_ref, gain_ref, wq_ref, out_hbm, gt_hbm, gq_ref, gw_ref, gg_ref, sem):
+    moves = []
+    for i, (src, dst) in enumerate(((out_in, out_hbm), (gt_in, gt_hbm))):
+        for j in range(4):
+            part = pl.ds(j * (T // 4), T // 4)
+            cp = pltpu.make_async_copy(src.at[part, :], dst.at[part, :], sem.at[4 * i + j])
+            cp.start()
+            moves.append(cp)
+    eye = lax.broadcasted_iota(jnp.int32, (ROWS, ROWS), 0) == lax.broadcasted_iota(
+        jnp.int32, (ROWS, ROWS), 1)
+    gain = jnp.sum(
+        jnp.where(eye, jnp.broadcast_to(gain_ref[...].astype(F32), (ROWS, ROWS)), 0.0),
+        axis=1, keepdims=True)
+    along = jnp.zeros((ROWS, 1), F32)
+    for h in range(NC):
+        part = s_ref[h][:ROWS, :WA_]
+        cols = slice(h * WA_, (h + 1) * WA_)
+        gq_ref[:, cols] = part * gain
+        along += jnp.sum(part * wq_ref[:, cols].astype(F32), axis=1, keepdims=True)
+        gw_ref[:, h * WB_:(h + 1) * WB_] = s_ref[h][:ROWS, WA_:]
+    gg_ref[...] = jnp.sum(
+        jnp.where(eye, jnp.broadcast_to(along, (ROWS, ROWS)), 0.0), axis=0, keepdims=True)
+    for cp in moves:
         cp.wait()
 
 
 def block_step(tokens, segment_ids, grad_out, norm_gain, w_qkv, w_out):
     any_, vm = pl.BlockSpec(memory_space=pl.ANY), pl.BlockSpec(memory_space=pltpu.VMEM)
     v = pltpu.VMEM
+    gain = norm_gain.reshape(1, ROWS)
     out, grad_tokens, sums = pl.pallas_call(
         kernel,
         out_shape=(
-            jax.ShapeDtypeStruct((T, D), BF),
-            jax.ShapeDtypeStruct((T, D), BF),
-            jax.ShapeDtypeStruct((NC, PAD, WX), F32),
+            pltpu.VMEM((T, D), BF),
+            pltpu.VMEM((T, D), BF),
+            pltpu.VMEM((NC, PAD, WX), F32),
         ),
         in_specs=[any_, any_, vm, vm, vm, vm],
-        out_specs=(any_, any_, vm),
+        out_specs=(vm, vm, vm),
         scratch_shapes=[
             v((NY, T, CH), BF), v((NY, T, CH), BF), v((NY, T, CH), BF),
             v((NY, CH, T), BF), v((NY, CH, T), BF), v((T, 128), F32),
@@ -552,24 +598,37 @@
             v((NC, T, WA_), F32), v((NC, T, WB_), BF), v((T, T), F32),
             v((T, HD), F32), v((T, HD), F32),
             v((5, T, HD), BF), v((T, HD), BF), v((4, T, T), BF),
-            v((NC, T, WB_), BF), v((NC, T, WA_), BF), v((NY, T, CH), BF), v((NY, T, CH), F32),
+            v((NC, T, WB_), BF), v((NC, T, WA_), BF), v((NY, T, CH), F32),
             v((NY, CH, WA_), BF), v((NY, CH, WA_), BF), v((NY, CH, WA_), BF),
             v((NZ, BLK, WA_), BF), v((2, NZ, BLK, WA_), BF), v((7, BLK, WA_), BF),
             v((NY, CH, WB_), BF), v((NY, CH, WB_), BF), v((NY, CH, WB_), BF),
-            v((2, 3, NY, BLK, WB_), BF), v((2, 2, BLK, WB_), BF), v((3, BLK, WB_), BF),
-            v((BLK + PAD, WX), F32), v((GROUP, PAD, WX), BF), v((GROUP, PAD, WX), BF),
-            pltpu.SemaphoreType.DMA((4 * NY,)),
+            v((3, CH, WB_), BF), v((NZ - 1, BLK, WB_), BF),
+            v((BLK + PAD, WA_), F32), v((BLK + PAD, WB_), F32),
+            v((GROUP, PAD, WA_), BF), v((GROUP, PAD, WA_), BF),
+            v((GROUP, PAD, WB_), BF), v((GROUP, PAD, WB_), BF),
+            pltpu.SemaphoreType.DMA((2 * NY,)),
             pltpu.SemaphoreType.DMA((N_COPIES,)), pltpu.SemaphoreType.DMA((N_COPIES,)),
+            pltpu.SemaphoreType.DMA((2 * GROUP,)),
         ],
         compiler_params=pltpu.CompilerParams(
-            collective_id=0, has_side_effects=True, vmem_limit_bytes=60 * 2 ** 20),
+            collective_id=0, has_side_effects=True, vmem_limit_bytes=50 * 2 ** 20),
         name="block_step",
-    )(tokens, grad_out, segment_ids, norm_gain.reshape(1, ROWS), w_qkv, w_out)
-    scaled_sum = jnp.concatenate([sums[0, :ROWS, :WA_], sums[1, :ROWS, :WA_]], axis=1)
-    out_sum = jnp.concatenate([sums[0, :ROWS, WA_:], sums[1, :ROWS, WA_:]], axis=1)
-    grad_qkv = scaled_sum * norm_gain.astype(F32)[:, None]
-    grad_gain = jnp.sum(scaled_sum * w_qkv.astype(F32), axis=1)
-    return out, grad_tokens, grad_qkv, out_sum.T, grad_gain
+    )(tokens, grad_out, segment_ids, gain, w_qkv, w_out.T)
+    out, grad_tokens, grad_qkv, grad_wout, grad_gain = pl.pallas_call(
+        finish_kernel,
+        out_shape=(
+            jax.ShapeDtypeStruct((T, D), BF),
+            jax.ShapeDtypeStruct((T, D), BF),
+            jax.ShapeDtypeStruct((ROWS, NC * WA_), F32),
+            jax.ShapeDtypeStruct((ROWS, NC * WB_), F32),
+            jax.ShapeDtypeStruct((1, ROWS), F32),
+        ),
+        in_specs=[vm, vm, vm, vm, vm],
+        out_specs=(any_, any_, vm, vm, vm),
+        scratch_shapes=[pltpu.SemaphoreType.DMA((8,))],
+        name="finish",
+    )(out, grad_tokens, sums, gain, w_qkv)
+    return out, grad_tokens, grad_qkv, grad_wout.T, grad_gain.reshape(ROWS)
 
 
 def solution(mesh):

time: 122 us -> 109 us (0.89)
  Pallas kernels: 111 us -> 102 us
  other arithmetic: 1.94 us -> 0 us
  local copies, waits for them, and re-layouts: 7.37 us -> 5.99 us
    pallas_call x1 -> x2, Pallas kernels: 111 us -> 102 us  [the longest x1 97.3 us: block_step(): pl.pallas_call(kernel, out_shape=(pltpu.VMEM((T, D), BF), pltpu.VMEM((T,...]
    squeeze x2 -> x0, local copies, waits for them, and re-layouts: 1.5 us -> none  [the longest x1 0.76 us: block_step(): sums[0, :ROWS, :WA_]]
    reduce_sum x1 -> x0, other arithmetic: 1.32 us -> none  [block_step(): grad_gain = jnp.sum(scaled_sum * w_qkv.astype(F32), axis=1)]
    unnamed x9 -> x14, local copies, waits for them, and re-layouts: 5.87 us -> 5.99 us
where the time goes in v2:
time: 109 us
  Pallas kernels  102 us (94%)
  local copies, waits for them, and re-layouts  5.99 us (5%)
    pallas_call x1, Pallas kernels, block_step(): pl.pallas_call(kernel, out_shape=(pltpu.VMEM((T, D), BF), pltpu.VMEM((T,...  97.3 us
    unnamed x14, local copies, waits for them, and re-layouts  5.99 us
    pallas_call x1, Pallas kernels, block_step(): pl.pallas_call(finish_kernel, out_shape=(jax.ShapeDtypeStruct((T, D), BF)...  4.77 us

profile of v2, /device:TPU:1, one launch (start us, length us, event | category | flops | bytes accessed | tf_op | source)
XLA Modules:
  0.0 108.9 jit_solution(10046607720441293338)
XLA Ops:
  0.6 0.0 copy-start.2
  0.6 0.7 copy-done.2
  1.4 0.0 copy-start.4
  1.4 0.7 copy-done.4
  2.1 0.0 copy-start.5
  2.1 0.7 copy-done.5
  2.7 0.0 copy-start.6
  2.7 0.7 copy-done.6
  3.4 97.3 %block_step.1 = (bf16[384,2560]{1,0:T(8,128)(2,1)S(1)}, bf16[384,2560]{1,0:T(8,128)(2,1)S(1)}, f32[2,16,640]{2,1,0:T(8,128)S(1)}) custom-call(bf16[384,2560]{1,0:T(8,128)(2,1)} %tok_hbm.1, bf16[384,2560]{1,0:T(8,128)(2,1)} %go_hbm.1, s32[1,384]{1,0:T(1,128)S(1)} %copy-done.6, bf16[1,10]{1,0:T(2,128)(2,1)S(1)} %bitcast.6, bf16[10,768]{1,0:T(8,128)(2,1)S(1)} %copy-done.2, ...), custom_call_target="tpu_custom_call" | custom-call | tf_op jit(solution)/shard_map/block_step/pallas_call | solution.py:584
  100.7 0.0 copy-start
  100.7 1.3 %copy-done = bf16[384,2560]{1,0:T(8,128)(2,1)} copy-done((bf16[384,2560]{1,0:T(8,128)(2,1)}, bf16[384,2560]{1,0:T(8,128)(2,1)S(1)}, u32[]{:S(2)}) %copy-start) | copy-done | bytes 1966104
  102.0 0.0 copy-start.1
  102.0 1.3 %copy-done.1 = bf16[384,2560]{1,0:T(8,128)(2,1)} copy-done((bf16[384,2560]{1,0:T(8,128)(2,1)}, bf16[384,2560]{1,0:T(8,128)(2,1)S(1)}, u32[]{:S(2)}) %copy-start.1) | copy-done | bytes 1966104
  103.3 0.0 copy-start.3
  103.3 0.6 copy-done.3
  103.9 4.8 %finish.1 = (bf16[384,2560]{1,0:T(8,128)(2,1)}, bf16[384,2560]{1,0:T(8,128)(2,1)}, f32[10,768]{1,0:T(8,128)}, f32[10,512]{1,0:T(8,128)}, f32[1,10]{1,0:T(1,128)}) custom-call(bf16[384,2560]{1,0:T(8,128)(2,1)} %copy-done, bf16[384,2560]{1,0:T(8,128)(2,1)} %copy-done.1, f32[2,16,640]{2,1,0:T(8,128)} %copy-done.3, bf16[1,10]{1,0:T(2,128)(2,1)} %bitcast.5, ...), custom_call_target="tpu_custom_call" | custom-call | tf_op jit(solution)/shard_map/finish/pallas_call | solution.py:617
Async XLA Ops:
  0.6 0.7 copy-start.2
  1.4 0.7 copy-start.4
  2.1 0.7 copy-start.5
  2.7 0.7 copy-start.6
  100.7 1.3 %copy-start = (bf16[384,2560]{1,0:T(8,128)(2,1)}, bf16[384,2560]{1,0:T(8,128)(2,1)S(1)}, u32[]{:S(2)}) copy-start(bf16[384,2560]{1,0:T(8,128)(2,1)S(1)} %get-tuple-element.13.out_in) | copy-start | bytes 5898244
  102.0 1.3 %copy-start.1 = (bf16[384,2560]{1,0:T(8,128)(2,1)}, bf16[384,2560]{1,0:T(8,128)(2,1)S(1)}, u32[]{:S(2)}) copy-start(bf16[384,2560]{1,0:T(8,128)(2,1)S(1)} %get-tuple-element.14.gt_in) | copy-start | bytes 5898244
  103.3 0.6 copy-start.3

commit v3 on v2

--- a/solution.py
+++ b/solution.py
@@ -33,10 +33,11 @@
 
 
 def kernel(
-    tok_hbm, go_hbm, seg_ref, gain_ref, wq_ref, wo_ref,
+    tok_hbm, go_hbm, seg_hbm, gain_hbm, wq_hbm, wo_hbm,
     out_ref, gt_ref, s_ref,
+    seg_ref, gain_ref, wq_ref, wo_ref,
     tok, go, sc, scT, goT, rr, blk, xg, tmp, wa, wb, proj, gm, mask, cs, sn,
-    qb, kv, pb, mx, dpr, gs,
+    qb, kb, kv, pb, mx, dpr, gs,
     ta, sa, ra, ya1, ya2, za, tb, sb, rb, xb, zb, fin, finb, xs, xr, xsb, xrb,
     lsem, ssem, rsem, fsem,
 ):
@@ -81,6 +82,13 @@
         copies.append(copy)
         return copy
 
+    small = []
+    for i, (src, dst) in enumerate(
+            ((gain_hbm, gain_ref), (wq_hbm, wq_ref), (wo_hbm, wo_ref), (seg_hbm, seg_ref))):
+        cp = pltpu.make_async_copy(src, dst, lsem.at[2 * NY + i])
+        cp.start()
+        small.append(cp)
+
     barrier = pltpu.get_barrier_semaphore()
 
     def greet(d):
@@ -108,6 +116,8 @@
             cp.start()
             loads.append(cp)
 
+    for cp in small:
+        cp.wait()
     diag = lax.broadcasted_iota(jnp.int32, (PAD, ROWS), 0) == lax.broadcasted_iota(
         jnp.int32, (PAD, ROWS), 1)
     gain_diag = jnp.where(diag, jnp.broadcast_to(gain_ref[...].astype(F32), (PAD, ROWS)), 0.0)
@@ -215,50 +225,56 @@
     cs[...] = jnp.cos(angles)
     sn[...] = jnp.where(lane < HD // 2, -1.0, 1.0) * jnp.sin(angles)
 
-    for cp in yb_c:
-        cp.wait_recv()
     zA_wait(1)
     zA(2)
     yA(1)
     yA(2)
-    for k in (1, 7, 2, 6, 3, 5, 4):
-        zB(k)
+    for cp in yb_c:
+        cp.wait_recv()
+    zB(1)
+    zB(7)
+    yA_forward(0)
     transpose(sc, scT, 0)
-    yA_forward(0)
     zA_wait(2)
     zA(3)
     yA(3)
     yA(4)
-    transpose(sc, scT, 1)
+    zB(2)
+    zB(6)
     yA_forward(1)
     yA_forward(2)
+    transpose(sc, scT, 1)
     zA_wait(3)
     zA(4)
     yA(5)
     yA(6)
+    zB(3)
+    zB(5)
     xB(1)
     xB(7)
-    transpose(sc, scT, 2)
     yA_forward(3)
     yA_forward(4)
+    transpose(sc, scT, 2)
     zA_wait(4)
     yA(7)
     pa_own = send(wa.at[c, y], wa.at[c, y], partner)
+    zB(4)
     xB(2)
     xB(6)
-    transpose(sc, scT, 3)
     yA_forward(5)
     yA_forward(6)
+    transpose(sc, scT, 3)
     for j in range(NY):
         loads[NY + j].wait()
-    xB(3)
-    xB(5)
-    xB(4)
+    transpose(go, goT, 0)
+    transpose(go, goT, 1)
     yA_forward(7)
     pa_l = send(wa.at[c, ym(-1)], wa.at[c, ym(-1)], partner)
     pa_r = send(wa.at[c, ym(1)], wa.at[c, ym(1)], partner)
-    for j in range(NY):
-        transpose(go, goT, j)
+    xB(3)
+    xB(5)
+    transpose(go, goT, 2)
+    transpose(go, goT, 3)
 
     def project(yy, first_one=False):
         left = sc[yy]
@@ -269,18 +285,23 @@
     pa_own.wait_recv()
     project(y, True)
     pa_f = []
-    for j in range(4):
+
+    def last_chunk(j):
         ya_f[j].wait_recv()
         b = ablk(ym(2), zm(offs[j]))
         pa_f.append(send(b, b, partner))
+
+    for j in range(4):
+        last_chunk(j)
     pa_l.wait_recv()
     project(ym(-1))
-    for j in range(4, 8):
-        ya_f[j].wait_recv()
-        b = ablk(ym(2), zm(offs[j]))
-        pa_f.append(send(b, b, partner))
+    xB(4)
+    last_chunk(4)
+    last_chunk(5)
     pa_r.wait_recv()
     project(ym(1))
+    last_chunk(6)
+    last_chunk(7)
     for cp in pa_f:
         cp.wait_recv()
     project(ym(2))
@@ -291,24 +312,29 @@
     def turn(v):
         return v * cs[...] + pltpu.roll(v, HD // 2, 1) * sn[...]
 
-    def unturn(v):
-        return v * cs[...] + pltpu.roll(v * sn[...], HD // 2, 1)
+    def four(block):
+        return jnp.concatenate([block] * 4, axis=0)
 
     for h in range(5):
         hf, col = head_cols(h)
         v = proj[hf, :, col:col + HD]
-        qb[h] = turn(v * rms(v)).astype(BF)
+        t = turn(v * rms(v)).astype(BF)
+        if h == 4:
+            kb[...] = t
+        else:
+            for i in range(3):
+                qb[i, h * 128:(h + 1) * 128, :] = t[i * 128:(i + 1) * 128]
     kv[...] = proj[1, :, 2 * HD:].astype(BF)
     scale = HD ** -0.5
-    for h in range(4):
-        for i in range(3):
-            r0, n = slice(i * 128, (i + 1) * 128), (i + 1) * 128
-            s = mm(qb[h, r0, :], qb[4, :n, :], NT) * scale
-            w = jnp.exp(s) * mask[r0, :n]
-            p = (w / jnp.sum(w, axis=-1, keepdims=True)).astype(BF)
-            pb[h, r0, :n] = p
-            mx[h // 2, r0, (h % 2) * HD:(h % 2 + 1) * HD] = mm(p, kv[:n, :]).astype(BF)
-        if h == 1:
+    for i in range(3):
+        r0, n = slice(i * 128, (i + 1) * 128), (i + 1) * 128
+        w = jnp.exp(mm(qb[i], kb[:n, :], NT) * scale) * four(mask[r0, :n])
+        p = (w * (1.0 / jnp.sum(w, axis=-1, keepdims=True))).astype(BF)
+        pb[i, :, :n] = p
+        mixed = mm(p, kv[:n, :]).astype(BF)
+        for h in range(4):
+            mx[h // 2, r0, (h % 2) * HD:(h % 2 + 1) * HD] = mixed[h * 128:(h + 1) * 128]
+        if i == 1:
             for cp in xb_c:
                 cp.wait_recv()
             pb_s = [send(wb.at[c, j], wb.at[c, j], partner) for j in range(NY)]
@@ -317,20 +343,14 @@
     for j in range(NY):
         sb[j] = mm(goT[j], mx[o]).astype(BF)
         rb_s.append(send(sb.at[j], rb.at[j], partner))
-    for j in range(NY):
-        tb[j] = mm(goT[j], mx[c]).astype(BF)
     for cp in pb_s:
         cp.wait_recv()
     for h in range(NC):
-        gm[h] = sum(mm(go[j], wb[h, j]) for j in range(NY)).astype(BF)
-    for j in range(NY):
-        rb_s[j].wait_recv()
-        tb[j] = (tb[j].astype(F32) + rb[j].astype(F32)).astype(BF)
-
-    xb_s = []
-    for m in (1, 3, 2):
-        t = lax.rem(xi + m, NX)
-        xb_s.append(send(tb.at[t], xb.at[m - 1], xdev(m)))
+        part = sum(mm(go[j], wb[h, j]) for j in range(NY)).astype(BF)
+        for i in range(3):
+            for k in range(2):
+                gm[i, (2 * h + k) * 128:(2 * h + k + 1) * 128, :] = (
+                    part[i * 128:(i + 1) * 128, k * HD:(k + 1) * HD])
 
     def add_into(ref, *others):
         total = ref[...].astype(F32)
@@ -338,38 +358,48 @@
             total = total + other[...].astype(F32)
         ref[...] = total.astype(BF)
 
-    def head_back(h, dk, dv):
-        dq = []
-        for i in range(3):
-            r0, n = slice(i * 128, (i + 1) * 128), (i + 1) * 128
-            do = gm[h // 2, r0, (h % 2) * HD:(h % 2 + 1) * HD]
-            dp = mm(do, kv[:n, :], NT)
-            p = pb[h, r0, :n]
-            pf = p.astype(F32)
-            delta = jnp.sum(pf * dp, axis=-1, keepdims=True)
-            ds = (pf * (dp - delta) * scale).astype(BF)
-            dq.append(mm(ds, qb[4, :n, :]))
-            tk = mm(ds, qb[h, r0, :], TN)
-            tv = mm(p, do, TN)
-            for m in range(i + 1):
-                dk[m] = dk[m] + tk[m * 128:(m + 1) * 128]
-                dv[m] = dv[m] + tv[m * 128:(m + 1) * 128]
-        return jnp.concatenate(dq, axis=0)
-
-    def project_back(h, d):
-        hf, col = head_cols(h)
-        v = proj[hf, :, col:col + HD]
+    xb_s = []
+
+    def start_x():
+        for j in range(NY):
+            tb[j] = mm(goT[j], mx[c]).astype(BF)
+        for j in range(NY):
+            rb_s[j].wait_recv()
+            add_into(tb.at[j], rb.at[j])
+        for m in (1, 3, 2):
+            t = lax.rem(xi + m, NX)
+            xb_s.append(send(tb.at[t], xb.at[m - 1], xdev(m)))
+
+    def norm_back(v, d, cos, sin):
         r = rms(v)
         xn = v * r
-        dn = unturn(d)
-        grad = r * (dn - xn * jnp.mean(dn * xn, axis=-1, keepdims=True))
-        dpr[hf, :, col:col + HD] = grad.astype(BF)
+        dn = d * cos + pltpu.roll(d * sin, HD // 2, 1)
+        return (r * (dn - xn * jnp.mean(dn * xn, axis=-1, keepdims=True))).astype(BF)
 
     dk = [jnp.zeros((128, HD), F32)] * 3
     dv = [jnp.zeros((128, HD), F32)] * 3
-    for h in range(4):
-        project_back(h, head_back(h, dk, dv))
-    project_back(4, jnp.concatenate(dk, axis=0))
+    for i in range(3):
+        r0, n = slice(i * 128, (i + 1) * 128), (i + 1) * 128
+        do = gm[i]
+        p = pb[i, :, :n]
+        pf = p.astype(F32)
+        dp = mm(do, kv[:n, :], NT)
+        delta = jnp.sum(pf * dp, axis=-1, keepdims=True)
+        ds = (pf * (dp - delta) * scale).astype(BF)
+        tk = mm(ds, qb[i], TN)
+        tv = mm(p, do, TN)
+        for m in range(i + 1):
+            dk[m] = dk[m] + tk[m * 128:(m + 1) * 128]
+            dv[m] = dv[m] + tv[m * 128:(m + 1) * 128]
+        v = jnp.concatenate(
+            [proj[h // 3, r0, (h % 3) * HD:(h % 3 + 1) * HD] for h in range(4)], axis=0)
+        grad = norm_back(v, mm(ds, kb[:n, :]), four(cs[r0, :]), four(sn[r0, :]))
+        for h in range(4):
+            dpr[h // 3, r0, (h % 3) * HD:(h % 3 + 1) * HD] = grad[h * 128:(h + 1) * 128]
+        if i == 0:
+            start_x()
+    dpr[1, :, HD:2 * HD] = norm_back(
+        proj[1, :, HD:2 * HD], jnp.concatenate(dk, axis=0), cs[...], sn[...])
     dpr[1, :, 2 * HD:] = jnp.concatenate(dv, axis=0).astype(BF)
 
     ra_s = {}
@@ -469,39 +499,35 @@
         def _():
             self_copy().start()
 
+    out_chunk(0)
+    out_chunk(1)
     step2(0)
-    out_chunk(0)
     step2(1)
-    out_chunk(1)
+    out_chunk(2)
     step2(2)
-    out_chunk(2)
-    sum_x()
     step2(3)
     out_chunk(3)
+    step2(4)
+    step2(5)
     ra_s[0].wait_recv()
     add_into(ta.at[y], ra.at[y])
-    step2(4)
-    step2(5)
     gs_chunk(0)
-    step3(0)
-    step_z(0)
     step2(6)
     step2(7)
     gs_chunk(1)
+    step3(0)
+    step_z(0)
+    gs_chunk(2)
+    sum_x()
     step3(1)
     step3(2)
     step_z(1)
     step_z(2)
-    gs_chunk(2)
+    gs_chunk(3)
     step3(3)
     step3(4)
     step_z(3)
     step_z(4)
-    gs_chunk(3)
-    step3(5)
-    step3(6)
-    step_z(5)
-    step_z(6)
 
     def token_rows(i, _):
         r0 = pl.ds(pl.multiple_of(i * 16, 16), 16)
@@ -514,7 +540,11 @@
             gt_ref[r0, j * CH:(j + 1) * CH] = (go[j, r0, :].astype(F32) + path).astype(BF)
         return 0
 
-    lax.fori_loop(0, T // 16, token_rows, 0, unroll=2)
+    lax.fori_loop(0, 8, token_rows, 0, unroll=2)
+    step3(5)
+    step3(6)
+    step_z(5)
+    step_z(6)
     sum_z()
     step3(7)
     sz[3].wait_recv()
@@ -530,6 +560,7 @@
         t = lax.rem(me8 + p, GROUP)
         last.append(send(xs.at[t], xr.at[me8], base + t))
     xr[me8] = xs[me8]
+    lax.fori_loop(8, T // 16, token_rows, 0, unroll=2)
     for i in range(GROUP):
         pltpu.make_async_copy(xsb.at[i], xrb.at[i], fsem.at[GROUP + i]).wait()
     for h in range(NC):
@@ -579,6 +610,7 @@
 
 def block_step(tokens, segment_ids, grad_out, norm_gain, w_qkv, w_out):
     any_, vm = pl.BlockSpec(memory_space=pl.ANY), pl.BlockSpec(memory_space=pltpu.VMEM)
+    hbm = pl.BlockSpec(memory_space=pltpu.HBM)
     v = pltpu.VMEM
     gain = norm_gain.reshape(1, ROWS)
     out, grad_tokens, sums = pl.pallas_call(
@@ -588,16 +620,17 @@
             pltpu.VMEM((T, D), BF),
             pltpu.VMEM((NC, PAD, WX), F32),
         ),
-        in_specs=[any_, any_, vm, vm, vm, vm],
+        in_specs=[hbm] * 6,
         out_specs=(vm, vm, vm),
         scratch_shapes=[
+            v((1, T), jnp.int32), v((1, ROWS), BF), v((ROWS, NC * WA_), BF), v((ROWS, NC * WB_), BF),
             v((NY, T, CH), BF), v((NY, T, CH), BF), v((NY, T, CH), BF),
             v((NY, CH, T), BF), v((NY, CH, T), BF), v((T, 128), F32),
             v((NC, PAD, WX), BF), v((GROUP, PAD, WX), BF), v((BLK, WX), F32),
             v((NC, NY, CH, WA_), BF), v((NC, NY, CH, WB_), BF),
-            v((NC, T, WA_), F32), v((NC, T, WB_), BF), v((T, T), F32),
+            v((NC, T, WA_), F32), v((3, 512, HD), BF), v((T, T), F32),
             v((T, HD), F32), v((T, HD), F32),
-            v((5, T, HD), BF), v((T, HD), BF), v((4, T, T), BF),
+            v((3, 512, HD), BF), v((T, HD), BF), v((T, HD), BF), v((3, 512, T), BF),
             v((NC, T, WB_), BF), v((NC, T, WA_), BF), v((NY, T, CH), F32),
             v((NY, CH, WA_), BF), v((NY, CH, WA_), BF), v((NY, CH, WA_), BF),
             v((NZ, BLK, WA_), BF), v((2, NZ, BLK, WA_), BF), v((7, BLK, WA_), BF),
@@ -606,12 +639,12 @@
             v((BLK + PAD, WA_), F32), v((BLK + PAD, WB_), F32),
             v((GROUP, PAD, WA_), BF), v((GROUP, PAD, WA_), BF),
             v((GROUP, PAD, WB_), BF), v((GROUP, PAD, WB_), BF),
-            pltpu.SemaphoreType.DMA((2 * NY,)),
+            pltpu.SemaphoreType.DMA((2 * NY + 4,)),
             pltpu.SemaphoreType.DMA((N_COPIES,)), pltpu.SemaphoreType.DMA((N_COPIES,)),
             pltpu.SemaphoreType.DMA((2 * GROUP,)),
         ],
         compiler_params=pltpu.CompilerParams(
-            collective_id=0, has_side_effects=True, vmem_limit_bytes=50 * 2 ** 20),
+            collective_id=0, has_side_effects=True, vmem_limit_bytes=55 * 2 ** 20),
         name="block_step",
     )(tokens, grad_out, segment_ids, gain, w_qkv, w_out.T)
     out, grad_tokens, grad_qkv, grad_wout, grad_gain = pl.pallas_call(
@@ -626,6 +659,7 @@
         in_specs=[vm, vm, vm, vm, vm],
         out_specs=(any_, any_, vm, vm, vm),
         scratch_shapes=[pltpu.SemaphoreType.DMA((8,))],
+        compiler_params=pltpu.CompilerParams(vmem_limit_bytes=8 * 2 ** 20),
         name="finish",
     )(out, grad_tokens, sums, gain, w_qkv)
     return out, grad_tokens, grad_qkv, grad_wout.T, grad_gain.reshape(ROWS)

time: 109 us -> 94.2 us (0.86)
  Pallas kernels: 102 us -> 93.3 us
  local copies, waits for them, and re-layouts: 5.99 us -> 0.01 us
    pallas_call x1, Pallas kernels: 97.3 us -> 90.7 us  [block_step(): pl.pallas_call(kernel, out_shape=(pltpu.VMEM((T, D), BF), pltpu.VMEM((T,...]
    unnamed x14 -> x4, local copies, waits for them, and re-layouts: 5.99 us -> 0.01 us
    pallas_call x1, Pallas kernels: 4.77 us -> 2.62 us  [block_step(): pl.pallas_call(finish_kernel, out_shape=(jax.ShapeDtypeStruct((T, D), BF)...]
where the time goes in v3:
time: 94.2 us; the launch traced here: 94.1 us
  Pallas kernels  93.3 us (99%)
    pallas_call x1, Pallas kernels, block_step(): pl.pallas_call(kernel, out_shape=(pltpu.VMEM((T, D), BF), pltpu.VMEM((T,...  90.7 us
    pallas_call x1, Pallas kernels, block_step(): pl.pallas_call(finish_kernel, out_shape=(jax.ShapeDtypeStruct((T, D), BF)...  2.62 us

profile of v3, /device:TPU:1, one launch (start us, length us, event | category | flops | bytes accessed | tf_op | source)
XLA Modules:
  0.0 94.1 jit_solution(6313824809173596156)
XLA Ops:
  0.6 0.0 copy-start
  0.6 0.0 copy-start.1
  0.7 90.7 %block_step.1 = (bf16[384,2560]{1,0:T(8,128)(2,1)S(1)}, bf16[384,2560]{1,0:T(8,128)(2,1)S(1)}, f32[2,16,640]{2,1,0:T(8,128)S(1)}) custom-call(bf16[384,2560]{1,0:T(8,128)(2,1)} %tok_hbm.1, bf16[384,2560]{1,0:T(8,128)(2,1)} %go_hbm.1, s32[1,384]{1,0:T(1,128)} %seg_hbm.1, bf16[1,10]{1,0:T(2,128)(2,1)} %bitcast.4, bf16[10,768]{1,0:T(8,128)(2,1)} %wq_ref.1, ...), custom_call_target="tpu_custom_call" | custom-call | tf_op jit(solution)/shard_map/block_step/pallas_call | solution.py:616
  91.3 0.0 copy-done
  91.3 0.0 copy-done.1
  91.4 2.6 %finish.1 = (bf16[384,2560]{1,0:T(8,128)(2,1)}, bf16[384,2560]{1,0:T(8,128)(2,1)}, f32[10,768]{1,0:T(8,128)}, f32[10,512]{1,0:T(8,128)}, f32[1,10]{1,0:T(1,128)}) custom-call(bf16[384,2560]{1,0:T(8,128)(2,1)S(1)} %get-tuple-element.13.out_in, bf16[384,2560]{1,0:T(8,128)(2,1)S(1)} %get-tuple-element.14.gt_in, f32[2,16,640]{2,1,0:T(8,128)S(1)} %get-tuple-element.15.s_ref, ...), custom_call_target="tpu_custom_call" | custom-call | tf_op jit(solution)/shard_map/finish/pallas_call | solution.py:650
Async XLA Ops:
  0.6 90.7 %copy-start = (bf16[10,768]{1,0:T(8,128)(2,1)S(1)}, bf16[10,768]{1,0:T(8,128)(2,1)}, u32[]{:S(2)}) copy-start(bf16[10,768]{1,0:T(8,128)(2,1)} %wq_ref.1) | copy-start | bytes 46084
  0.6 90.7 %copy-start.1 = (bf16[10]{0:T(256)(128)(2,1)S(1)}, bf16[10]{0:T(256)(128)(2,1)}, u32[]{:S(2)}) copy-start(bf16[10]{0:T(256)(128)(2,1)} %param.9) | copy-start | bytes 64

commit v4 on v3

--- a/solution.py
+++ b/solution.py
@@ -15,6 +15,7 @@
 CH = NZ * BLK
 WA_, WB_ = 384, 256
 WX = WA_ + WB_
+W1, W2 = 256, 128
 PAD = 16
 EPS = 1e-06
 LOG_BASE = math.log(1000000.0)
@@ -38,7 +39,7 @@
     seg_ref, gain_ref, wq_ref, wo_ref,
     tok, go, sc, scT, goT, rr, blk, xg, tmp, wa, wb, proj, gm, mask, cs, sn,
     qb, kb, kv, pb, mx, dpr, gs,
-    ta, sa, ra, ya1, ya2, za, tb, sb, rb, xb, zb, fin, finb, xs, xr, xsb, xrb,
+    ta, sa, ra, ya1, ya2, za, zc, yc, tb, sb, rb, xb, zb, fin, finb, xs, xr, xsb, xrb,
     lsem, ssem, rsem, fsem,
 ):
     idx = lax.axis_index("dp")
@@ -199,7 +200,7 @@
         zb_c[k].wait_recv()
         b = bblk(xi, zm(-k))
         for m in (1, 3, 2):
-            xb_c.append(send(b, b, xdev(m)))
+            xb_c.append((m, send(b, b, xdev(m))))
 
     def transpose(src, dst, j):
         for k in range(CH // 128):
@@ -250,6 +251,7 @@
     yA(6)
     zB(3)
     zB(5)
+    zB(4)
     xB(1)
     xB(7)
     yA_forward(3)
@@ -258,21 +260,22 @@
     zA_wait(4)
     yA(7)
     pa_own = send(wa.at[c, y], wa.at[c, y], partner)
-    zB(4)
     xB(2)
     xB(6)
+    transpose(sc, scT, 3)
     yA_forward(5)
+    xB(3)
+    xB(5)
     yA_forward(6)
-    transpose(sc, scT, 3)
     for j in range(NY):
         loads[NY + j].wait()
     transpose(go, goT, 0)
     transpose(go, goT, 1)
+    xB(4)
     yA_forward(7)
     pa_l = send(wa.at[c, ym(-1)], wa.at[c, ym(-1)], partner)
     pa_r = send(wa.at[c, ym(1)], wa.at[c, ym(1)], partner)
-    xB(3)
-    xB(5)
+    pb_s = [send(wb.at[c, xi], wb.at[c, xi], partner)]
     transpose(go, goT, 2)
     transpose(go, goT, 3)
 
@@ -295,7 +298,6 @@
         last_chunk(j)
     pa_l.wait_recv()
     project(ym(-1))
-    xB(4)
     last_chunk(4)
     last_chunk(5)
     pa_r.wait_recv()
@@ -335,9 +337,12 @@
         for h in range(4):
             mx[h // 2, r0, (h % 2) * HD:(h % 2 + 1) * HD] = mixed[h * 128:(h + 1) * 128]
         if i == 1:
-            for cp in xb_c:
-                cp.wait_recv()
-            pb_s = [send(wb.at[c, j], wb.at[c, j], partner) for j in range(NY)]
+            for m in (1, 3, 2):
+                for mm_, cp in xb_c:
+                    if mm_ == m:
+                        cp.wait_recv()
+                b = wb.at[c, lax.rem(xi + NX - m, NX)]
+                pb_s.append(send(b, b, partner))
 
     rb_s = []
     for j in range(NY):
@@ -403,7 +408,8 @@
     dpr[1, :, 2 * HD:] = jnp.concatenate(dv, axis=0).astype(BF)
 
     ra_s = {}
-    for k in (2, 1, 3, 0):
+
+    def partial(k):
         yy = ym(k)
         sa[yy] = mm(scT[yy], dpr[o]).astype(BF)
         ra_s[k] = send(sa.at[yy], ra.at[yy], partner)
@@ -412,17 +418,52 @@
     roffs = [4, 3, -3, 2, -2, 1, -1, 0]
 
     def tblk(yy, j):
-        return ta.at[yy, rows(zm(roffs[j])), :]
-
-    s1, s2r, s2l, sz = {}, {}, {}, {}
+        return ta.at[yy, rows(zm(roffs[j])), pl.ds(0, W1)]
+
+    def thalf(h, k):
+        return ta.at[pl.ds(2 * h, 2), rows(zm(k)), pl.ds(W1, W2)]
+
+    s1, s2r, s2l, sz, zc_s = {}, {}, {}, {}, {}
+    partial(2)
+    partial(1)
     ra_s[2].wait_recv()
     for j in range(8):
-        add_into(tblk(ym(2), j), ra.at[ym(2), rows(zm(roffs[j])), :])
+        b = rows(zm(roffs[j]))
+        add_into(ta.at[ym(2), b, :], ra.at[ym(2), b, :])
         s1[j] = send(tblk(ym(2), j), ya1.at[j], right_y if j % 2 == 0 else left_y)
-    ra_s[1].wait_recv()
-    add_into(ta.at[ym(1)], ra.at[ym(1)])
-    ra_s[3].wait_recv()
-    add_into(ta.at[ym(3)], ra.at[ym(3)])
+    partial(3)
+    partial(0)
+    for k in (1, 3, 0):
+        ra_s[k].wait_recv()
+        add_into(ta.at[ym(k)], ra.at[ym(k)])
+
+    def zc_send(side, h, s):
+        zc_s[side, h, s] = send(
+            thalf(h, -s if side else s), zc.at[side, h, s - 1], left_z if side else right_z)
+
+    def zc_add(side, h, s):
+        zc_s[side, h, s + 1].wait_recv()
+        add_into(thalf(h, -s if side else s), zc.at[side, h, s])
+
+    def zc_round(n):
+        for side, h, s in ((0, 0, 4 - n), (1, 1, 4 - n), (0, 1, 3 - n), (1, 0, 3 - n)):
+            if s > 0:
+                zc_add(side, h, s)
+                zc_send(side, h, s)
+
+    def zc_end():
+        for h in range(2):
+            for side in range(2):
+                zc_s[side, h, 1].wait_recv()
+            add_into(thalf(h, 0), zc.at[0, h, 0], zc.at[1, h, 0])
+        return [
+            send(ta.at[ym(k), rows(z), pl.ds(W1, W2)], yc.at[k - 1], dev(ym(k), z))
+            for k in (2, 1, 3)]
+
+    zc_send(0, 0, 4)
+    zc_send(1, 1, 4)
+    zc_send(0, 1, 3)
+    zc_send(1, 0, 3)
 
     def step2(j):
         s1[j].wait_recv()
@@ -503,26 +544,28 @@
     out_chunk(1)
     step2(0)
     step2(1)
+    zc_round(1)
     out_chunk(2)
     step2(2)
     step2(3)
     out_chunk(3)
+    zc_round(2)
     step2(4)
     step2(5)
-    ra_s[0].wait_recv()
-    add_into(ta.at[y], ra.at[y])
     gs_chunk(0)
     step2(6)
     step2(7)
+    zc_round(3)
     gs_chunk(1)
     step3(0)
     step_z(0)
     gs_chunk(2)
-    sum_x()
+    yc_s = zc_end()
     step3(1)
     step3(2)
     step_z(1)
     step_z(2)
+    sum_x()
     gs_chunk(3)
     step3(3)
     step3(4)
@@ -545,11 +588,15 @@
     step3(6)
     step_z(5)
     step_z(6)
-    sum_z()
+    lax.fori_loop(8, 16, token_rows, 0, unroll=2)
     step3(7)
+    for cp in yc_s:
+        cp.wait_recv()
+    fin[:BLK, W1:] = ta[y, rows(z), W1:].astype(F32) + sum(
+        yc[k].astype(F32) for k in range(NY - 1))
     sz[3].wait_recv()
     sz[6].wait_recv()
-    fin[:BLK, :] = (
+    fin[:BLK, :W1] = (
         tblk(y, 7)[...].astype(F32) + za[3].astype(F32) + za[6].astype(F32))
     fin[BLK:, :] = jnp.zeros((PAD, WA_), F32)
 
@@ -560,7 +607,8 @@
         t = lax.rem(me8 + p, GROUP)
         last.append(send(xs.at[t], xr.at[me8], base + t))
     xr[me8] = xs[me8]
-    lax.fori_loop(8, T // 16, token_rows, 0, unroll=2)
+    sum_z()
+    lax.fori_loop(16, T // 16, token_rows, 0, unroll=2)
     for i in range(GROUP):
         pltpu.make_async_copy(xsb.at[i], xrb.at[i], fsem.at[GROUP + i]).wait()
     for h in range(NC):
@@ -633,7 +681,8 @@
             v((3, 512, HD), BF), v((T, HD), BF), v((T, HD), BF), v((3, 512, T), BF),
             v((NC, T, WB_), BF), v((NC, T, WA_), BF), v((NY, T, CH), F32),
             v((NY, CH, WA_), BF), v((NY, CH, WA_), BF), v((NY, CH, WA_), BF),
-            v((NZ, BLK, WA_), BF), v((2, NZ, BLK, WA_), BF), v((7, BLK, WA_), BF),
+            v((NZ, BLK, W1), BF), v((2, NZ, BLK, W1), BF), v((7, BLK, W1), BF),
+            v((2, 2, 4, 2, BLK, W2), BF), v((NY - 1, BLK, W2), BF),
             v((NY, CH, WB_), BF), v((NY, CH, WB_), BF), v((NY, CH, WB_), BF),
             v((3, CH, WB_), BF), v((NZ - 1, BLK, WB_), BF),
             v((BLK + PAD, WA_), F32), v((BLK + PAD, WB_), F32),

time: 94.2 us -> 94.6 us (level)
  no operation moved by 1% of the time
where the time goes in v4:
time: 94.6 us; the launch traced here: 94.5 us
  Pallas kernels  93.7 us (99%)
    pallas_call x1, Pallas kernels, block_step(): pl.pallas_call(kernel, out_shape=(pltpu.VMEM((T, D), BF), pltpu.VMEM((T,...  91.1 us
    pallas_call x1, Pallas kernels, block_step(): pl.pallas_call(finish_kernel, out_shape=(jax.ShapeDtypeStruct((T, D), BF)...  2.62 us

profile of v4, /device:TPU:1, one launch (start us, length us, event | category | flops | bytes accessed | tf_op | source)
XLA Modules:
  0.0 94.5 jit_solution(4088848860651223117)
XLA Ops:
  0.6 0.0 copy-start
  0.6 0.0 copy-start.1
  0.7 91.1 %block_step.1 = (bf16[384,2560]{1,0:T(8,128)(2,1)S(1)}, bf16[384,2560]{1,0:T(8,128)(2,1)S(1)}, f32[2,16,640]{2,1,0:T(8,128)S(1)}) custom-call(bf16[384,2560]{1,0:T(8,128)(2,1)} %tok_hbm.1, bf16[384,2560]{1,0:T(8,128)(2,1)} %go_hbm.1, s32[1,384]{1,0:T(1,128)} %seg_hbm.1, bf16[1,10]{1,0:T(2,128)(2,1)} %bitcast.4, bf16[10,768]{1,0:T(8,128)(2,1)} %wq_ref.1, ...), custom_call_target="tpu_custom_call" | custom-call | tf_op jit(solution)/shard_map/block_step/pallas_call | solution.py:664
  91.7 0.0 copy-done
  91.7 0.0 copy-done.1
  91.7 2.6 %finish.1 = (bf16[384,2560]{1,0:T(8,128)(2,1)}, bf16[384,2560]{1,0:T(8,128)(2,1)}, f32[10,768]{1,0:T(8,128)}, f32[10,512]{1,0:T(8,128)}, f32[1,10]{1,0:T(1,128)}) custom-call(bf16[384,2560]{1,0:T(8,128)(2,1)S(1)} %get-tuple-element.13.out_in, bf16[384,2560]{1,0:T(8,128)(2,1)S(1)} %get-tuple-element.14.gt_in, f32[2,16,640]{2,1,0:T(8,128)S(1)} %get-tuple-element.15.s_ref, ...), custom_call_target="tpu_custom_call" | custom-call | tf_op jit(solution)/shard_map/finish/pallas_call | solution.py:699
Async XLA Ops:
  0.6 91.1 %copy-start = (bf16[10,768]{1,0:T(8,128)(2,1)S(1)}, bf16[10,768]{1,0:T(8,128)(2,1)}, u32[]{:S(2)}) copy-start(bf16[10,768]{1,0:T(8,128)(2,1)} %wq_ref.1) | copy-start | bytes 46084
  0.6 91.1 %copy-start.1 = (bf16[10]{0:T(256)(128)(2,1)S(1)}, bf16[10]{0:T(256)(128)(2,1)}, u32[]{:S(2)}) copy-start(bf16[10]{0:T(256)(128)(2,1)} %param.9) | copy-start | bytes 64

commit v5 on v4

--- a/solution.py
+++ b/solution.py
@@ -38,7 +38,7 @@
     out_ref, gt_ref, s_ref,
     seg_ref, gain_ref, wq_ref, wo_ref,
     tok, go, sc, scT, goT, rr, blk, xg, tmp, wa, wb, proj, gm, mask, cs, sn,
-    qb, kb, kv, pb, mx, dpr, gs,
+    qb, kb, kv, pb, mx, dpr, dots,
     ta, sa, ra, ya1, ya2, za, zc, yc, tb, sb, rb, xb, zb, fin, finb, xs, xr, xsb, xrb,
     lsem, ssem, rsem, fsem,
 ):
@@ -344,10 +344,28 @@
                 b = wb.at[c, lax.rem(xi + NX - m, NX)]
                 pb_s.append(send(b, b, partner))
 
+    def add_into(ref, *others):
+        total = ref[...].astype(F32)
+        for other in others:
+            total = total + other[...].astype(F32)
+        ref[...] = total.astype(BF)
+
     rb_s = []
     for j in range(NY):
         sb[j] = mm(goT[j], mx[o]).astype(BF)
         rb_s.append(send(sb.at[j], rb.at[j], partner))
+    for j in range(NY):
+        tb[j] = mm(goT[j], mx[c]).astype(BF)
+    for j in range(NY):
+        rb_s[j].wait_recv()
+        add_into(tb.at[j], rb.at[j])
+
+    xb_s = []
+    for q in range(2):
+        cols = pl.ds(q * W2, W2)
+        for m in (1, 3, 2):
+            t = lax.rem(xi + m, NX)
+            xb_s.append(send(tb.at[t, :, cols], xb.at[m - 1, :, cols], xdev(m)))
     for cp in pb_s:
         cp.wait_recv()
     for h in range(NC):
@@ -356,24 +374,6 @@
             for k in range(2):
                 gm[i, (2 * h + k) * 128:(2 * h + k + 1) * 128, :] = (
                     part[i * 128:(i + 1) * 128, k * HD:(k + 1) * HD])
-
-    def add_into(ref, *others):
-        total = ref[...].astype(F32)
-        for other in others:
-            total = total + other[...].astype(F32)
-        ref[...] = total.astype(BF)
-
-    xb_s = []
-
-    def start_x():
-        for j in range(NY):
-            tb[j] = mm(goT[j], mx[c]).astype(BF)
-        for j in range(NY):
-            rb_s[j].wait_recv()
-            add_into(tb.at[j], rb.at[j])
-        for m in (1, 3, 2):
-            t = lax.rem(xi + m, NX)
-            xb_s.append(send(tb.at[t], xb.at[m - 1], xdev(m)))
 
     def norm_back(v, d, cos, sin):
         r = rms(v)
@@ -401,8 +401,6 @@
         grad = norm_back(v, mm(ds, kb[:n, :]), four(cs[r0, :]), four(sn[r0, :]))
         for h in range(4):
             dpr[h // 3, r0, (h % 3) * HD:(h % 3 + 1) * HD] = grad[h * 128:(h + 1) * 128]
-        if i == 0:
-            start_x()
     dpr[1, :, HD:2 * HD] = norm_back(
         proj[1, :, HD:2 * HD], jnp.concatenate(dk, axis=0), cs[...], sn[...])
     dpr[1, :, 2 * HD:] = jnp.concatenate(dv, axis=0).astype(BF)
@@ -497,17 +495,28 @@
         update = sum(mm(mx[h], wb[h, j], NT) for h in range(NC))
         out_ref[:, j * CH:(j + 1) * CH] = (tok[j].astype(F32) + update).astype(BF)
 
-    def gs_chunk(j):
-        gs[j] = sum(mm(dpr[h], wa[h, j], NT) for h in range(NC))
+    def row_dots():
+        total = sum(
+            jnp.sum(dpr[h].astype(F32) * proj[h], axis=-1, keepdims=True) for h in range(NC))
+        dots[...] = jnp.broadcast_to(total * (1.0 / D), (T, 128))
+
+    def gt_chunk(j):
+        r = rr[...][:, :1]
+        g = sum(mm(dpr[h], wa[h, j], NT) for h in range(NC))
+        path = (r * (g - tok[j].astype(F32) * (r * dots[...][:, :1]))).astype(BF)
+        gt_ref[:, j * CH:(j + 1) * CH] = (
+            go[j].astype(F32) + path.astype(F32)).astype(BF)
 
     zb_s = []
 
-    def sum_x():
-        for cp in xb_s:
+    def sum_x(q):
+        cols = pl.ds(q * W2, W2)
+        for cp in xb_s[3 * q:3 * q + 3]:
             cp.wait_recv()
-        add_into(tb.at[xi], xb.at[0], xb.at[1], xb.at[2])
+        add_into(tb.at[xi, :, cols], *[xb.at[m, :, cols] for m in range(3)])
         for k in (4, 3, 5, 2, 6, 1, 7):
-            zb_s.append(send(tb.at[xi, rows(zm(k)), :], zb.at[k - 1], dev(y, zm(k))))
+            zb_s.append(send(
+                tb.at[xi, rows(zm(k)), cols], zb.at[k - 1, :, cols], dev(y, zm(k))))
 
     def piece_copy(p):
         t = lax.rem(me8 + p, GROUP)
@@ -540,11 +549,13 @@
         def _():
             self_copy().start()
 
+    row_dots()
     out_chunk(0)
     out_chunk(1)
     step2(0)
     step2(1)
     zc_round(1)
+    sum_x(0)
     out_chunk(2)
     step2(2)
     step2(3)
@@ -552,44 +563,32 @@
     zc_round(2)
     step2(4)
     step2(5)
-    gs_chunk(0)
+    gt_chunk(0)
     step2(6)
     step2(7)
     zc_round(3)
-    gs_chunk(1)
+    gt_chunk(1)
     step3(0)
     step_z(0)
-    gs_chunk(2)
+    gt_chunk(2)
     yc_s = zc_end()
+    sum_x(1)
     step3(1)
     step3(2)
     step_z(1)
     step_z(2)
-    sum_x()
-    gs_chunk(3)
+    gt_chunk(3)
     step3(3)
     step3(4)
     step_z(3)
     step_z(4)
 
-    def token_rows(i, _):
-        r0 = pl.ds(pl.multiple_of(i * 16, 16), 16)
-        r = rr[r0, :][:, :1]
-        xn = [tok[j, r0, :].astype(F32) * r for j in range(NY)]
-        g = [gs[j, r0, :] for j in range(NY)]
-        dot = sum(jnp.sum(a * b, axis=-1, keepdims=True) for a, b in zip(xn, g)) * (1.0 / D)
-        for j in range(NY):
-            path = (r * (g[j] - xn[j] * dot)).astype(BF).astype(F32)
-            gt_ref[r0, j * CH:(j + 1) * CH] = (go[j, r0, :].astype(F32) + path).astype(BF)
-        return 0
-
-    lax.fori_loop(0, 8, token_rows, 0, unroll=2)
     step3(5)
     step3(6)
     step_z(5)
     step_z(6)
-    lax.fori_loop(8, 16, token_rows, 0, unroll=2)
     step3(7)
+    sum_z()
     for cp in yc_s:
         cp.wait_recv()
     fin[:BLK, W1:] = ta[y, rows(z), W1:].astype(F32) + sum(
@@ -607,8 +606,6 @@
         t = lax.rem(me8 + p, GROUP)
         last.append(send(xs.at[t], xr.at[me8], base + t))
     xr[me8] = xs[me8]
-    sum_z()
-    lax.fori_loop(16, T // 16, token_rows, 0, unroll=2)
     for i in range(GROUP):
         pltpu.make_async_copy(xsb.at[i], xrb.at[i], fsem.at[GROUP + i]).wait()
     for h in range(NC):
@@ -679,7 +676,7 @@
             v((NC, T, WA_), F32), v((3, 512, HD), BF), v((T, T), F32),
             v((T, HD), F32), v((T, HD), F32),
             v((3, 512, HD), BF), v((T, HD), BF), v((T, HD), BF), v((3, 512, T), BF),
-            v((NC, T, WB_), BF), v((NC, T, WA_), BF), v((NY, T, CH), F32),
+            v((NC, T, WB_), BF), v((NC, T, WA_), BF), v((T, 128), F32),
             v((NY, CH, WA_), BF), v((NY, CH, WA_), BF), v((NY, CH, WA_), BF),
             v((NZ, BLK, W1), BF), v((2, NZ, BLK, W1), BF), v((7, BLK, W1), BF),
             v((2, 2, 4, 2, BLK, W2), BF), v((NY - 1, BLK, W2), BF),

time: 94.6 us -> 95.4 us (level)
  no operation moved by 1% of the time
where the time goes in v5:
time: 95.4 us; the launch traced here: 95.3 us
  Pallas kernels  94.5 us (99%)
    pallas_call x1, Pallas kernels, block_step(): pl.pallas_call(kernel, out_shape=(pltpu.VMEM((T, D), BF), pltpu.VMEM((T,...  91.9 us
    pallas_call x1, Pallas kernels, block_step(): pl.pallas_call(finish_kernel, out_shape=(jax.ShapeDtypeStruct((T, D), BF)...  2.62 us

profile of v5, /device:TPU:1, one launch (start us, length us, event | category | flops | bytes accessed | tf_op | source)
XLA Modules:
  0.0 95.3 jit_solution(4455446210097814836)
XLA Ops:
  0.6 0.0 copy-start
  0.6 0.0 copy-start.1
  0.7 91.9 %block_step.1 = (bf16[384,2560]{1,0:T(8,128)(2,1)S(1)}, bf16[384,2560]{1,0:T(8,128)(2,1)S(1)}, f32[2,16,640]{2,1,0:T(8,128)S(1)}) custom-call(bf16[384,2560]{1,0:T(8,128)(2,1)} %tok_hbm.1, bf16[384,2560]{1,0:T(8,128)(2,1)} %go_hbm.1, s32[1,384]{1,0:T(1,128)} %seg_hbm.1, bf16[1,10]{1,0:T(2,128)(2,1)} %bitcast.4, bf16[10,768]{1,0:T(8,128)(2,1)} %wq_ref.1, ...), custom_call_target="tpu_custom_call" | custom-call | tf_op jit(solution)/shard_map/block_step/pallas_call | solution.py:661
  92.5 0.0 copy-done
  92.5 0.0 copy-done.1
  92.5 2.6 %finish.1 = (bf16[384,2560]{1,0:T(8,128)(2,1)}, bf16[384,2560]{1,0:T(8,128)(2,1)}, f32[10,768]{1,0:T(8,128)}, f32[10,512]{1,0:T(8,128)}, f32[1,10]{1,0:T(1,128)}) custom-call(bf16[384,2560]{1,0:T(8,128)(2,1)S(1)} %get-tuple-element.13.out_in, bf16[384,2560]{1,0:T(8,128)(2,1)S(1)} %get-tuple-element.14.gt_in, f32[2,16,640]{2,1,0:T(8,128)S(1)} %get-tuple-element.15.s_ref, ...), custom_call_target="tpu_custom_call" | custom-call | tf_op jit(solution)/shard_map/finish/pallas_call | solution.py:696
Async XLA Ops:
  0.6 91.9 %copy-start = (bf16[10,768]{1,0:T(8,128)(2,1)S(1)}, bf16[10,768]{1,0:T(8,128)(2,1)}, u32[]{:S(2)}) copy-start(bf16[10,768]{1,0:T(8,128)(2,1)} %wq_ref.1) | copy-start | bytes 46084
  0.6 91.9 %copy-start.1 = (bf16[10]{0:T(256)(128)(2,1)S(1)}, bf16[10]{0:T(256)(128)(2,1)}, u32[]{:S(2)}) copy-start(bf16[10]{0:T(256)(128)(2,1)} %param.9) | copy-start | bytes 64

commit v6 on v5

--- a/solution.py
+++ b/solution.py
@@ -15,7 +15,7 @@
 CH = NZ * BLK
 WA_, WB_ = 384, 256
 WX = WA_ + WB_
-W1, W2 = 256, 128
+W2 = 128
 PAD = 16
 EPS = 1e-06
 LOG_BASE = math.log(1000000.0)
@@ -39,7 +39,7 @@
     seg_ref, gain_ref, wq_ref, wo_ref,
     tok, go, sc, scT, goT, rr, blk, xg, tmp, wa, wb, proj, gm, mask, cs, sn,
     qb, kb, kv, pb, mx, dpr, dots,
-    ta, sa, ra, ya1, ya2, za, zc, yc, tb, sb, rb, xb, zb, fin, finb, xs, xr, xsb, xrb,
+    ta, sa, ra, ya1, ya2, za, tb, sb, rb, xb, zb, fin, finb, xs, xr, xsb, xrb,
     lsem, ssem, rsem, fsem,
 ):
     idx = lax.axis_index("dp")
@@ -234,44 +234,44 @@
         cp.wait_recv()
     zB(1)
     zB(7)
+    zB(2)
+    zB(6)
     yA_forward(0)
-    transpose(sc, scT, 0)
     zA_wait(2)
     zA(3)
     yA(3)
     yA(4)
-    zB(2)
-    zB(6)
-    yA_forward(1)
-    yA_forward(2)
-    transpose(sc, scT, 1)
-    zA_wait(3)
-    zA(4)
-    yA(5)
-    yA(6)
     zB(3)
     zB(5)
     zB(4)
     xB(1)
     xB(7)
+    yA_forward(1)
+    yA_forward(2)
+    transpose(sc, scT, 0)
+    zA_wait(3)
+    zA(4)
+    yA(5)
+    yA(6)
+    xB(2)
+    xB(6)
     yA_forward(3)
     yA_forward(4)
-    transpose(sc, scT, 2)
+    transpose(sc, scT, 1)
     zA_wait(4)
     yA(7)
     pa_own = send(wa.at[c, y], wa.at[c, y], partner)
-    xB(2)
-    xB(6)
-    transpose(sc, scT, 3)
-    yA_forward(5)
     xB(3)
     xB(5)
+    transpose(sc, scT, 2)
+    yA_forward(5)
+    xB(4)
     yA_forward(6)
+    transpose(sc, scT, 3)
     for j in range(NY):
         loads[NY + j].wait()
     transpose(go, goT, 0)
     transpose(go, goT, 1)
-    xB(4)
     yA_forward(7)
     pa_l = send(wa.at[c, ym(-1)], wa.at[c, ym(-1)], partner)
     pa_r = send(wa.at[c, ym(1)], wa.at[c, ym(1)], partner)
@@ -354,18 +354,21 @@
     for j in range(NY):
         sb[j] = mm(goT[j], mx[o]).astype(BF)
         rb_s.append(send(sb.at[j], rb.at[j], partner))
-    for j in range(NY):
-        tb[j] = mm(goT[j], mx[c]).astype(BF)
-    for j in range(NY):
-        rb_s[j].wait_recv()
-        add_into(tb.at[j], rb.at[j])
+    def own_part():
+        for j in range(NY):
+            own = mm(goT[j], mx[c])
+            rb_s[j].wait_recv()
+            own = (own + rb[j].astype(F32)).astype(BF)
+            for q in range(2):
+                tb[q, j] = own[:, q * W2:(q + 1) * W2]
 
     xb_s = []
-    for q in range(2):
-        cols = pl.ds(q * W2, W2)
+
+    def start_x(q):
         for m in (1, 3, 2):
             t = lax.rem(xi + m, NX)
-            xb_s.append(send(tb.at[t, :, cols], xb.at[m - 1, :, cols], xdev(m)))
+            xb_s.append(send(tb.at[q, t], xb.at[q, m - 1], xdev(m)))
+
     for cp in pb_s:
         cp.wait_recv()
     for h in range(NC):
@@ -401,6 +404,9 @@
         grad = norm_back(v, mm(ds, kb[:n, :]), four(cs[r0, :]), four(sn[r0, :]))
         for h in range(4):
             dpr[h // 3, r0, (h % 3) * HD:(h % 3 + 1) * HD] = grad[h * 128:(h + 1) * 128]
+        if i == 0:
+            own_part()
+            start_x(0)
     dpr[1, :, HD:2 * HD] = norm_back(
         proj[1, :, HD:2 * HD], jnp.concatenate(dk, axis=0), cs[...], sn[...])
     dpr[1, :, 2 * HD:] = jnp.concatenate(dv, axis=0).astype(BF)
@@ -416,12 +422,10 @@
     roffs = [4, 3, -3, 2, -2, 1, -1, 0]
 
     def tblk(yy, j):
-        return ta.at[yy, rows(zm(roffs[j])), pl.ds(0, W1)]
-
-    def thalf(h, k):
-        return ta.at[pl.ds(2 * h, 2), rows(zm(k)), pl.ds(W1, W2)]
-
-    s1, s2r, s2l, sz, zc_s = {}, {}, {}, {}, {}
+        return ta.at[yy, rows(zm(roffs[j])), :]
+
+    s1, s2r, s2l, sz = {}, {}, {}, {}
+    start_x(1)
     partial(2)
     partial(1)
     ra_s[2].wait_recv()
@@ -435,34 +439,6 @@
         ra_s[k].wait_recv()
         add_into(ta.at[ym(k)], ra.at[ym(k)])
 
-    def zc_send(side, h, s):
-        zc_s[side, h, s] = send(
-            thalf(h, -s if side else s), zc.at[side, h, s - 1], left_z if side else right_z)
-
-    def zc_add(side, h, s):
-        zc_s[side, h, s + 1].wait_recv()
-        add_into(thalf(h, -s if side else s), zc.at[side, h, s])
-
-    def zc_round(n):
-        for side, h, s in ((0, 0, 4 - n), (1, 1, 4 - n), (0, 1, 3 - n), (1, 0, 3 - n)):
-            if s > 0:
-                zc_add(side, h, s)
-                zc_send(side, h, s)
-
-    def zc_end():
-        for h in range(2):
-            for side in range(2):
-                zc_s[side, h, 1].wait_recv()
-            add_into(thalf(h, 0), zc.at[0, h, 0], zc.at[1, h, 0])
-        return [
-            send(ta.at[ym(k), rows(z), pl.ds(W1, W2)], yc.at[k - 1], dev(ym(k), z))
-            for k in (2, 1, 3)]
-
-    zc_send(0, 0, 4)
-    zc_send(1, 1, 4)
-    zc_send(0, 1, 3)
-    zc_send(1, 0, 3)
-
     def step2(j):
         s1[j].wait_recv()
         add_into(tblk(ym(1) if j % 2 == 0 else ym(3), j), ya1.at[j])
@@ -477,8 +453,6 @@
     def step_z(j):
         if j == 0:
             sz[0] = send(tblk(y, 0), za.at[0], right_z)
-        elif j == 7:
-            return
         elif j % 2 == 1:
             n = (j + 1) // 2
             sz[n - 1].wait_recv()
@@ -510,13 +484,12 @@
     zb_s = []
 
     def sum_x(q):
-        cols = pl.ds(q * W2, W2)
         for cp in xb_s[3 * q:3 * q + 3]:
             cp.wait_recv()
-        add_into(tb.at[xi, :, cols], *[xb.at[m, :, cols] for m in range(3)])
+        add_into(tb.at[q, xi], *[xb.at[q, m] for m in range(3)])
         for k in (4, 3, 5, 2, 6, 1, 7):
             zb_s.append(send(
-                tb.at[xi, rows(zm(k)), cols], zb.at[k - 1, :, cols], dev(y, zm(k))))
+                tb.at[q, xi, rows(zm(k)), :], zb.at[q, k - 1], dev(y, zm(k))))
 
     def piece_copy(p):
         t = lax.rem(me8 + p, GROUP)
@@ -533,8 +506,9 @@
     def sum_z():
         for cp in zb_s:
             cp.wait_recv()
-        finb[:BLK, :] = tb[xi, rows(z), :].astype(F32) + sum(
-            zb[k].astype(F32) for k in range(NZ - 1))
+        for q in range(2):
+            finb[:BLK, q * W2:(q + 1) * W2] = tb[q, xi, rows(z), :].astype(F32) + sum(
+                zb[q, k].astype(F32) for k in range(NZ - 1))
         finb[BLK:, :] = jnp.zeros((PAD, WB_), F32)
         for i in range(GROUP):
             xsb[i] = finb[i * ROWS:i * ROWS + PAD, :].astype(BF)
@@ -551,51 +525,43 @@
 
     row_dots()
     out_chunk(0)
-    out_chunk(1)
     step2(0)
     step2(1)
-    zc_round(1)
     sum_x(0)
-    out_chunk(2)
     step2(2)
     step2(3)
-    out_chunk(3)
-    zc_round(2)
+    step3(0)
+    step_z(0)
     step2(4)
     step2(5)
-    gt_chunk(0)
-    step2(6)
-    step2(7)
-    zc_round(3)
-    gt_chunk(1)
-    step3(0)
-    step_z(0)
-    gt_chunk(2)
-    yc_s = zc_end()
-    sum_x(1)
     step3(1)
     step3(2)
     step_z(1)
     step_z(2)
-    gt_chunk(3)
+    step2(6)
+    step2(7)
+    sum_x(1)
+    out_chunk(1)
     step3(3)
     step3(4)
     step_z(3)
     step_z(4)
-
+    out_chunk(2)
+    out_chunk(3)
+    gt_chunk(0)
     step3(5)
     step3(6)
     step_z(5)
     step_z(6)
+    gt_chunk(1)
+    gt_chunk(2)
+    gt_chunk(3)
+    sum_z()
     step3(7)
-    sum_z()
-    for cp in yc_s:
-        cp.wait_recv()
-    fin[:BLK, W1:] = ta[y, rows(z), W1:].astype(F32) + sum(
-        yc[k].astype(F32) for k in range(NY - 1))
+    gt_chunk(3)
     sz[3].wait_recv()
     sz[6].wait_recv()
-    fin[:BLK, :W1] = (
+    fin[:BLK, :] = (
         tblk(y, 7)[...].astype(F32) + za[3].astype(F32) + za[6].astype(F32))
     fin[BLK:, :] = jnp.zeros((PAD, WA_), F32)
 
@@ -678,10 +644,9 @@
             v((3, 512, HD), BF), v((T, HD), BF), v((T, HD), BF), v((3, 512, T), BF),
             v((NC, T, WB_), BF), v((NC, T, WA_), BF), v((T, 128), F32),
             v((NY, CH, WA_), BF), v((NY, CH, WA_), BF), v((NY, CH, WA_), BF),
-            v((NZ, BLK, W1), BF), v((2, NZ, BLK, W1), BF), v((7, BLK, W1), BF),
-            v((2, 2, 4, 2, BLK, W2), BF), v((NY - 1, BLK, W2), BF),
-            v((NY, CH, WB_), BF), v((NY, CH, WB_), BF), v((NY, CH, WB_), BF),
-            v((3, CH, WB_), BF), v((NZ - 1, BLK, WB_), BF),
+            v((NZ, BLK, WA_), BF), v((2, NZ, BLK, WA_), BF), v((7, BLK, WA_), BF),
+            v((2, NY, CH, W2), BF), v((NY, CH, WB_), BF), v((NY, CH, WB_), BF),
+            v((2, 3, CH, W2), BF), v((2, NZ - 1, BLK, W2), BF),
             v((BLK + PAD, WA_), F32), v((BLK + PAD, WB_), F32),
             v((GROUP, PAD, WA_), BF), v((GROUP, PAD, WA_), BF),
             v((GROUP, PAD, WB_), BF), v((GROUP, PAD, WB_), BF),

time: 95.4 us -> 90.5 us (0.949)
  Pallas kernels: 94.5 us -> 89.6 us
    pallas_call x1, Pallas kernels: 91.9 us -> 87 us  [block_step(): pl.pallas_call(kernel, out_shape=(pltpu.VMEM((T, D), BF), pltpu.VMEM((T,...]
where the time goes in v6:
time: 90.5 us; the launch traced here: 90.4 us
  Pallas kernels  89.6 us (99%)
    pallas_call x1, Pallas kernels, block_step(): pl.pallas_call(kernel, out_shape=(pltpu.VMEM((T, D), BF), pltpu.VMEM((T,...  87 us
    pallas_call x1, Pallas kernels, block_step(): pl.pallas_call(finish_kernel, out_shape=(jax.ShapeDtypeStruct((T, D), BF)...  2.62 us

profile of v6, /device:TPU:1, one launch (start us, length us, event | category | flops | bytes accessed | tf_op | source)
XLA Modules:
  0.0 90.4 jit_solution(11582148135314054041)
XLA Ops:
  0.6 0.0 copy-start
  0.6 0.0 copy-start.1
  0.7 87.0 %block_step.1 = (bf16[384,2560]{1,0:T(8,128)(2,1)S(1)}, bf16[384,2560]{1,0:T(8,128)(2,1)S(1)}, f32[2,16,640]{2,1,0:T(8,128)S(1)}) custom-call(bf16[384,2560]{1,0:T(8,128)(2,1)} %tok_hbm.1, bf16[384,2560]{1,0:T(8,128)(2,1)} %go_hbm.1, s32[1,384]{1,0:T(1,128)} %seg_hbm.1, bf16[1,10]{1,0:T(2,128)(2,1)} %bitcast.4, bf16[10,768]{1,0:T(8,128)(2,1)} %wq_ref.1, ...), custom_call_target="tpu_custom_call" | custom-call | tf_op jit(solution)/shard_map/block_step/pallas_call | solution.py:627
  87.6 0.0 copy-done
  87.6 0.0 copy-done.1
  87.6 2.6 %finish.1 = (bf16[384,2560]{1,0:T(8,128)(2,1)}, bf16[384,2560]{1,0:T(8,128)(2,1)}, f32[10,768]{1,0:T(8,128)}, f32[10,512]{1,0:T(8,128)}, f32[1,10]{1,0:T(1,128)}) custom-call(bf16[384,2560]{1,0:T(8,128)(2,1)S(1)} %get-tuple-element.13.out_in, bf16[384,2560]{1,0:T(8,128)(2,1)S(1)} %get-tuple-element.14.gt_in, f32[2,16,640]{2,1,0:T(8,128)S(1)} %get-tuple-element.15.s_ref, ...), custom_call_target="tpu_custom_call" | custom-call | tf_op jit(solution)/shard_map/finish/pallas_call | solution.py:661
Async XLA Ops:
  0.6 87.0 %copy-start = (bf16[10,768]{1,0:T(8,128)(2,1)S(1)}, bf16[10,768]{1,0:T(8,128)(2,1)}, u32[]{:S(2)}) copy-start(bf16[10,768]{1,0:T(8,128)(2,1)} %wq_ref.1) | copy-start | bytes 46084
  0.6 87.0 %copy-start.1 = (bf16[10]{0:T(256)(128)(2,1)S(1)}, bf16[10]{0:T(256)(128)(2,1)}, u32[]{:S(2)}) copy-start(bf16[10]{0:T(256)(128)(2,1)} %param.9) | copy-start | bytes 64

commit v7 on v6

--- a/solution.py
+++ b/solution.py
@@ -527,9 +527,9 @@
     out_chunk(0)
     step2(0)
     step2(1)
-    sum_x(0)
     step2(2)
     step2(3)
+    sum_x(0)
     step3(0)
     step_z(0)
     step2(4)
@@ -540,12 +540,12 @@
     step_z(2)
     step2(6)
     step2(7)
-    sum_x(1)
     out_chunk(1)
     step3(3)
     step3(4)
     step_z(3)
     step_z(4)
+    sum_x(1)
     out_chunk(2)
     out_chunk(3)
     gt_chunk(0)

time: 90.5 us -> 90.3 us (level)
  no operation moved by 1% of the time
where the time goes in v7:
time: 90.3 us; the launch traced here: 90.1 us
  Pallas kernels  89.3 us (99%)
    pallas_call x1, Pallas kernels, block_step(): pl.pallas_call(kernel, out_shape=(pltpu.VMEM((T, D), BF), pltpu.VMEM((T,...  86.7 us
    pallas_call x1, Pallas kernels, block_step(): pl.pallas_call(finish_kernel, out_shape=(jax.ShapeDtypeStruct((T, D), BF)...  2.62 us

profile of v7, /device:TPU:1, one launch (start us, length us, event | category | flops | bytes accessed | tf_op | source)
XLA Modules:
  0.0 90.1 jit_solution(15934975895958941139)
XLA Ops:
  0.6 0.0 copy-start
  0.6 0.0 copy-start.1
  0.7 86.7 %block_step.1 = (bf16[384,2560]{1,0:T(8,128)(2,1)S(1)}, bf16[384,2560]{1,0:T(8,128)(2,1)S(1)}, f32[2,16,640]{2,1,0:T(8,128)S(1)}) custom-call(bf16[384,2560]{1,0:T(8,128)(2,1)} %tok_hbm.1, bf16[384,2560]{1,0:T(8,128)(2,1)} %go_hbm.1, s32[1,384]{1,0:T(1,128)} %seg_hbm.1, bf16[1,10]{1,0:T(2,128)(2,1)} %bitcast.4, bf16[10,768]{1,0:T(8,128)(2,1)} %wq_ref.1, ...), custom_call_target="tpu_custom_call" | custom-call | tf_op jit(solution)/shard_map/block_step/pallas_call | solution.py:627
  87.3 0.0 copy-done
  87.4 0.0 copy-done.1
  87.4 2.6 %finish.1 = (bf16[384,2560]{1,0:T(8,128)(2,1)}, bf16[384,2560]{1,0:T(8,128)(2,1)}, f32[10,768]{1,0:T(8,128)}, f32[10,512]{1,0:T(8,128)}, f32[1,10]{1,0:T(1,128)}) custom-call(bf16[384,2560]{1,0:T(8,128)(2,1)S(1)} %get-tuple-element.13.out_in, bf16[384,2560]{1,0:T(8,128)(2,1)S(1)} %get-tuple-element.14.gt_in, f32[2,16,640]{2,1,0:T(8,128)S(1)} %get-tuple-element.15.s_ref, ...), custom_call_target="tpu_custom_call" | custom-call | tf_op jit(solution)/shard_map/finish/pallas_call | solution.py:661
Async XLA Ops:
  0.6 86.7 %copy-start = (bf16[10,768]{1,0:T(8,128)(2,1)S(1)}, bf16[10,768]{1,0:T(8,128)(2,1)}, u32[]{:S(2)}) copy-start(bf16[10,768]{1,0:T(8,128)(2,1)} %wq_ref.1) | copy-start | bytes 46084
  0.6 86.7 %copy-start.1 = (bf16[10]{0:T(256)(128)(2,1)S(1)}, bf16[10]{0:T(256)(128)(2,1)}, u32[]{:S(2)}) copy-start(bf16[10]{0:T(256)(128)(2,1)} %param.9) | copy-start | bytes 64
